TPU v7x, 768 devices: a whole 4x8x12 slice. The times are simulated.
768 devices in a mesh: dp: 64 (over x, y, z_hi), enc: 12 (over z_lo, core).
Axes of the slice: x: 4, y: 8, z: 12 (z_hi: 2, z_lo: 6; z = z_hi * 6 + z_lo), core: 2. Of those that a mesh axis runs over, the one named last changes fastest.
Arguments:
- patches: bfloat16 [3072, 196, 768], P(('dp', 'enc')), may hold values from -6 to 6
- item_counts: int32 [768], P(('dp', 'enc')), may hold values from 1 to 4, as said below
- item_ids: int32 [3072], P(('dp', 'enc')), may hold values from 0 to 65535
- block_dest: int32 [12288], P(('dp', 'enc')), may hold values from 0 to 11, as said below
- enc_weight: bfloat16 [12, 768, 768], P('enc'), may hold values from -0.21875 to 0.21875
- enc_bias: float32 [12, 768], P('enc'), may hold values from -3 to 3
- enc_gain: float32 [12, 768], P('enc'), may hold values from 0.5 to 1.5
- item_bias: float32 [65536], replicated, may hold values from -2 to 2
- user_state: bfloat16 [196608, 768], P(('dp', 'enc')), may hold values from -6 to 6
- user_proj: bfloat16 [768, 768], replicated, may hold values from -0.21875 to 0.21875
- positives: int32 [196608], P(('dp', 'enc')), may hold values from 0 to 999
Outputs:
- d_user_state: bfloat16 [196608, 768], P(('dp', 'enc'))
- grad_weight: float32 [12, 768, 768], P('enc', 'dp')
- grad_bias: float32 [12, 768], P('enc')
- grad_gain: float32 [12, 768], P('enc')
Inputs may be any that keep to these rules, and one draw needn't show every extreme that they name: `item_counts`: live items of each device; device 0 holds 4. `block_dest`: among the blocks of one device at most 2 name the same expert; in every group of devices along enc some expert receives 2 live blocks from every device of the group.
All inputs are finite; a program needn't handle non-finite values.
Results may differ from a plain program's by a relative error of at most 0.017.
Values may be sent and summed in bfloat16 or wider, within the bound.
A program may use at most 32 MiB of HBM per device.

v0:
```python
import jax
import jax.numpy as jnp
from jax import lax
from jax.sharding import PartitionSpec as P

D = 768
PATCH_IN = 768
PATCHES = 196
BLOCK_ROWS = 49
BLOCKS_ITEM = 4
ITEMS_DEV = 4


score_scale = 0.1
loss_weight = 16.0
norm_eps = 1e-05


def pooled_rows(projected, bias_rows, gain_rows):
    shifted = projected + bias_rows
    center = jnp.mean(shifted, axis=-1, keepdims=True)
    deviation = shifted - center
    variance = jnp.mean(deviation * deviation, axis=-1, keepdims=True)
    normed = deviation * lax.rsqrt(variance + norm_eps) * gain_rows
    return jnp.sum(jax.nn.gelu(normed, approximate=True), axis=-2)


def body(
    patches,
    item_counts,
    item_ids,
    block_dest,
    enc_weight,
    enc_bias,
    enc_gain,
    item_bias,
    user_state,
    user_proj,
    positives,
):
    n_enc = lax.axis_size("enc")
    n_dp = lax.axis_size("dp")
    blocks_dev = ITEMS_DEV * BLOCKS_ITEM
    capacity = max(2, (blocks_dev + n_enc - 1) // n_enc)
    slots = n_enc * capacity
    live_items = item_counts[0]
    blocks = patches.reshape(blocks_dev, BLOCK_ROWS * PATCH_IN)
    live_block = jnp.arange(blocks_dev, dtype=jnp.int32) // BLOCKS_ITEM < live_items
    enc_index = jnp.arange(n_enc, dtype=jnp.int32)
    routed = ((block_dest[:, None] == enc_index[None, :]) & live_block[:, None]).astype(jnp.int32)
    rank_slot = jnp.cumsum(routed, axis=0) - routed
    slot_index = jnp.sum(routed * (enc_index[None, :] * capacity + rank_slot), axis=1)
    selector = (
        (jnp.arange(slots, dtype=jnp.int32)[:, None] == slot_index[None, :]) & live_block[None, :]
    ).astype(jnp.bfloat16)
    outgoing = jnp.dot(selector, blocks, preferred_element_type=jnp.float32).astype(jnp.bfloat16)
    outgoing = outgoing.reshape(n_enc, capacity, BLOCK_ROWS, PATCH_IN)
    weight = enc_weight[0]
    bias_vec = enc_bias[0]
    gain_vec = enc_gain[0]
    received = lax.all_to_all(outgoing, "enc", split_axis=0, concat_axis=0, tiled=True)
    projected = jnp.einsum("skrp,pd->skrd", received, weight, preferred_element_type=jnp.float32)
    received, projected = (received, projected)
    pooled_out, backward = jax.vjp(pooled_rows, projected, bias_vec, gain_vec)
    partial_value = pooled_out.astype(jnp.bfloat16)
    returned = lax.all_to_all(partial_value, "enc", split_axis=0, concat_axis=0, tiled=True)
    block_part = jnp.dot(selector.T, returned.reshape(slots, D), preferred_element_type=jnp.float32)
    summed = jnp.sum(block_part.reshape(ITEMS_DEV, BLOCKS_ITEM, D), axis=1)
    embed = (summed / PATCHES).astype(jnp.bfloat16)
    user_vec = jnp.dot(user_state, user_proj, preferred_element_type=jnp.float32).astype(
        jnp.bfloat16
    )
    catalogue = jnp.arange(item_bias.shape[0], dtype=jnp.int32)
    bias_items = jnp.sum(
        jnp.where(item_ids[:, None] == catalogue[None, :], item_bias[None, :], 0.0), axis=1
    )
    scores = (
        jnp.dot(user_vec, embed.T, preferred_element_type=jnp.float32) * score_scale
        + bias_items[None, :]
    )
    item_index = jnp.arange(ITEMS_DEV, dtype=jnp.int32)
    live_item = item_index < live_items
    target = (item_index[None, :] == (positives % live_items)[:, None]).astype(jnp.float32)
    d_score = jnp.where(
        live_item[None, :], loss_weight * (jax.nn.sigmoid(scores) - target), 0.0
    ).astype(jnp.bfloat16)
    d_embed = (
        jnp.dot(d_score.T, user_vec, preferred_element_type=jnp.float32) * score_scale
    ).astype(jnp.bfloat16)
    d_user_vec = (jnp.dot(d_score, embed, preferred_element_type=jnp.float32) * score_scale).astype(
        jnp.bfloat16
    )
    d_user = jnp.dot(d_user_vec, user_proj.T, preferred_element_type=jnp.float32).astype(
        jnp.bfloat16
    )
    d_block = jnp.repeat(d_embed, BLOCKS_ITEM, axis=0)
    grad_out = jnp.dot(selector, d_block, preferred_element_type=jnp.float32).astype(jnp.bfloat16)
    grad_out = grad_out.reshape(n_enc, capacity, D)
    grad_in = lax.all_to_all(grad_out, "enc", split_axis=0, concat_axis=0, tiled=True)
    d_part = grad_in.astype(jnp.float32) / PATCHES
    d_proj, d_bias, d_gain = backward(d_part)
    d_proj_low = d_proj.astype(jnp.bfloat16)
    grad_terms = jnp.einsum(
        "skrp,skrd->pd", received, d_proj_low, preferred_element_type=jnp.float32
    )
    total_w, total_b, total_g = lax.psum((grad_terms, d_bias, d_gain), "dp")
    row_count = PATCH_IN // n_dp
    mine = lax.dynamic_slice_in_dim(total_w, lax.axis_index("dp") * row_count, row_count, 0)
    return (d_user, (mine / n_dp)[None], (total_b / n_dp)[None], (total_g / n_dp)[None])


def solution(mesh):
    return jax.shard_map(
        body,
        mesh=mesh,
        in_specs=(
            P(("dp", "enc"), None, None),
            P(("dp", "enc")),
            P(("dp", "enc")),
            P(("dp", "enc")),
            P("enc", None, None),
            P("enc", None),
            P("enc", None),
            P(),
            P(("dp", "enc"), None),
            P(),
            P(("dp", "enc")),
        ),
        out_specs=(P(("dp", "enc"), None), P("enc", "dp", None), P("enc", None), P("enc", None)),
        check_vma=False,
    )
```

profile of v0, /device:TPU:6, one launch (start us, length us, event | category | flops | bytes accessed | tf_op | source)
XLA Modules:
  0.0 1176.1 jit_solution(1828424676419166478)
XLA Ops:
  7.2 0.0 copy-start
  7.2 0.0 copy-start.6
  8.0 1.4 copy.28
  9.4 2.4 reshape.126
  11.8 0.0 copy-done.6
  11.8 0.1 fusion.38
  11.9 0.2 select_reduce_fusion.1
  12.1 3.1 convolution_convert_fusion
  15.2 2.7 reshape.127
  17.9 0.0 copy-start.4
  18.0 0.0 copy-start.5
  18.0 0.0 copy-start.3
  18.0 0.0 copy-start.8
  18.0 0.0 copy-start.7
  18.0 2.6 copy.29
  20.6 12.1 %all-to-all-start = ((bf16[12,2,49,768]{3,1,2,0:T(2,128)(2,1)}), bf16[12,2,49,768]{3,1,2,0:T(2,128)(2,1)S(1)}, u32[]{:S(2)}, u32[]{:S(2)}) async-start(bf16[12,2,49,768]{3,1,2,0:T(2,128)(2,1)} %copy.29), calls=%async_computation | async-start | bytes 3612672 | tf_op jit(solution)/shard_map/all_to_all | solution.py:61
  32.8 0.1 eq.79
  32.9 0.0 copy-done.4
  32.9 0.0 copy-done.5
  32.9 0.0 copy-done.3
  33.0 0.0 copy-done.8
  33.0 0.9 select_reduce_fusion
  33.9 0.0 copy-done.7
  33.9 0.1 and_select_fusion
  34.0 1.9 convolution_convert_fusion.2
  35.9 60.0 %all-to-all-done = bf16[12,2,49,768]{3,1,2,0:T(2,128)(2,1)S(1)} async-done(((bf16[12,2,49,768]{3,1,2,0:T(2,128)(2,1)}), bf16[12,2,49,768]{3,1,2,0:T(2,128)(2,1)S(1)}, u32[]{:S(2)}, u32[]{:S(2)}) %all-to-all-start) | async-done | bytes 1806368 | tf_op jit(solution)/shard_map/all_to_all | solution.py:61
  95.9 0.0 copy-done
  95.9 1.9 add_reduce_fusion.1
  97.8 0.0 copy-start.1
  97.8 0.8 multiply_reduce_fusion.2
  98.6 1.1 copy-done.1
  99.7 2.9 fusion.7
  102.7 4.6 all-to-all-start.1
  107.3 0.0 all-reduce.3.cloned.1.call-start
  107.4 8.7 all-to-all-done.1
  116.1 0.2 convolution_reduce_fusion
  116.3 0.3 fusion.29
  116.6 0.2 fusion.20
  116.8 0.1 convolution_convert_fusion.3
  117.0 0.0 copy-start.2
  117.0 11.5 all_to_all.15
  128.5 0.1 convert_multiply_fusion.1
  128.6 5.8 multiply_reduce_fusion
  134.5 0.0 copy-done.2
  134.5 4.9 fusion.53
  139.4 0.5 add_reduce_fusion
  139.8 3.5 fusion.13
  143.3 0.0 all-reduce.3.cloned.1.call-update
  143.3 2.7 convolution_convert_fusion.1
  146.0 290.0 %all-reduce = (f32[768]{0:T(1024)S(1)}, f32[768]{0:T(1024)S(1)}) all-reduce(f32[768]{0:T(1024)S(1)} %get-tuple-element.26, f32[768]{0:T(1024)S(1)} %get-tuple-element.20), channel_id=1, replica_groups=mesh['dp'=64,'enc'=12] {'dp'}, use_global_device_ids=true, to_apply=%region_11.12 | all-reduce | flops 1536 | bytes 12288 | tf_op jit(solution)/shard_map/psum | solution.py:106
  436.0 0.6 broadcast_in_dim.70
  436.6 0.6 broadcast_in_dim.71
  437.2 730.5 %all-reduce.3.cloned.1.call-done = f32[768,768]{1,0:T(8,128)} async-done(((f32[768,768]{1,0:T(8,128)}), f32[768,768]{1,0:T(8,128)}) %all-reduce.3.cloned.1.call-update) | async-done | bytes 2359312 | tf_op jit(solution)/shard_map/psum | solution.py:106
  1167.7 0.9 multiply_bitcast_fusion
  1168.6 0.7 copy.33
  (16 shorter events, 0.2 us)
Async XLA Ops:
  7.2 88.7 %copy-start = (bf16[1,768,768]{2,1,0:T(8,128)(2,1)S(1)}, bf16[1,768,768]{2,1,0:T(8,128)(2,1)}, u32[]{:S(2)}) copy-start(bf16[1,768,768]{2,1,0:T(8,128)(2,1)} %param.15) | copy-start | bytes 3538948
  7.2 4.6 copy-start.6
  17.9 14.9 %copy-start.4 = (f32[1,768]{1,0:T(1,128)S(1)}, f32[1,768]{1,0:T(1,128)}, u32[]{:S(2)}) copy-start(f32[1,768]{1,0:T(1,128)} %param.16) | copy-start | bytes 9220
  18.0 14.9 %copy-start.5 = (f32[1,768]{1,0:T(1,128)S(1)}, f32[1,768]{1,0:T(1,128)}, u32[]{:S(2)}) copy-start(f32[1,768]{1,0:T(1,128)} %param.17) | copy-start | bytes 9220
  18.0 15.0 %copy-start.3 = (f32[65536]{0:T(1024)S(1)}, f32[65536]{0:T(1024)}, u32[]{:S(2)}) copy-start(f32[65536]{0:T(1024)} %param.18) | copy-start | bytes 786436
  18.0 15.0 %copy-start.8 = (s32[4]{0:T(128)S(1)}, s32[4]{0:T(128)}, u32[]{:S(2)}) copy-start(s32[4]{0:T(128)} %param.13) | copy-start | bytes 52
  18.0 15.9 %copy-start.7 = (s32[256]{0:T(256)S(1)}, s32[256]{0:T(256)}, u32[]{:S(2)}) copy-start(s32[256]{0:T(256)} %param.21) | copy-start | bytes 3076
  20.6 75.2 %all-to-all-start = ((bf16[12,2,49,768]{3,1,2,0:T(2,128)(2,1)}), bf16[12,2,49,768]{3,1,2,0:T(2,128)(2,1)S(1)}, u32[]{:S(2)}, u32[]{:S(2)}) async-start(bf16[12,2,49,768]{3,1,2,0:T(2,128)(2,1)} %copy.29), calls=%async_computation | async-start | bytes 3612672 | tf_op jit(solution)/shard_map/all_to_all | solution.py:61
  97.8 1.9 copy-start.1
  102.7 13.4 %all-to-all-start.1 = ((bf16[12,2,768]{2,1,0:T(2,128)(2,1)}), bf16[12,2,768]{2,1,0:T(2,128)(2,1)S(1)}, u32[]{:S(2)}, u32[]{:S(2)}) async-start(bf16[12,2,768]{2,1,0:T(2,128)(2,1)} %fusion.7), calls=%async_computation.1 | async-start | bytes 73728 | tf_op jit(solution)/shard_map/all_to_all | solution.py:66
  107.3 1060.3 %all-reduce.3.cloned.1.call-start = ((), (), s32[]{:S(2)}) async-start(), calls=%async_computation.3 | async-start | bytes 4718592 | tf_op jit(solution)/shard_map/psum | solution.py:106
  117.0 17.5 %copy-start.2 = (f32[12,2,49,768]{3,2,1,0:T(8,128)S(1)}, f32[12,2,49,768]{3,2,1,0:T(8,128)}, u32[]{:S(2)}) copy-start(f32[12,2,49,768]{3,2,1,0:T(8,128)} %copy-done.1) | copy-start | bytes 10838020
Sparse Core Ops, SparseCore 0:
  143.4 1024.2 all-reduce.2
where the time goes:
time: 1190 us; the launch traced here: 1180 us
  waiting for transfers between devices  799 us (67%)
  blocking collectives  302 us (25%)
  other arithmetic  17.3 us (1%)
  starting transfers between devices  16.8 us (1%)
  between operations  15.1 us (1%)
  matrix products  13.9 us (1%)
  local copies, waits for them, and re-layouts  12.3 us (1%)
    psum x1, waiting for transfers between devices, body(): total_w, total_b, total_g = lax.psum((grad_terms, d_bias, d_gain), 'dp')  730 us
    psum x1, blocking collectives, body(): total_w, total_b, total_g = lax.psum((grad_terms, d_bias, d_gain), 'dp')  290 us
    all_to_all x1, waiting for transfers between devices, body(): lax.all_to_all(outgoing, 'enc', split_axis=0, concat_axis=0, tiled=True)  60 us
  transfers between devices with their start and end apart: 3, of which 3 were waited for; matrix products, arithmetic and copies ran while one was open for 1% of the time, Pallas kernels for 0%

commit v1 on v0

--- a/solution.py
+++ b/solution.py
@@ -1,7 +1,13 @@
 import jax
 import jax.numpy as jnp
 from jax import lax
+from jax.experimental import pallas as pl
+from jax.experimental.pallas import tpu as pltpu
 from jax.sharding import PartitionSpec as P
+
+NX, NY, NZ = 4, 8, 2
+ROWS_DEV = 12
+FOLD = 1152
 
 D = 768
 PATCH_IN = 768
@@ -23,6 +29,147 @@
     variance = jnp.mean(deviation * deviation, axis=-1, keepdims=True)
     normed = deviation * lax.rsqrt(variance + norm_eps) * gain_rows
     return jnp.sum(jax.nn.gelu(normed, approximate=True), axis=-2)
+
+
+def fold(rows):
+    tail = rows[8:12]
+    return jnp.concatenate([rows[0:8], jnp.concatenate([tail[:, :384], tail[:, 384:]], axis=0)], axis=1)
+
+
+def unfold(folded):
+    tail = folded[:, 768:]
+    return jnp.concatenate([folded[:, :768], jnp.concatenate([tail[0:4], tail[4:8]], axis=1)], axis=0)
+
+
+def reduce_kernel(
+    g_ref, v_ref, out_ref, vout_ref,
+    sx, rx, sy, ry, accx, sz, rz, vx, vy, vz,
+    sem_sx, sem_rx, sem_sy, sem_ry, sem_z, sem_vsx, sem_vrx, sem_vsy, sem_vry, sem_vz,
+):
+    dp = lax.axis_index("dp")
+    x = dp // (NY * NZ)
+    y = (dp // NZ) % NY
+    z = dp % NZ
+
+    def at(xx, yy, zz):
+        return {"dp": (xx * NY + yy) * NZ + zz}
+
+    barrier = pltpu.get_barrier_semaphore()
+    for d in range(1, NX):
+        pl.semaphore_signal(barrier, inc=1, device_id=at((x + d) % NX, y, z))
+    for d in range(1, NY):
+        pl.semaphore_signal(barrier, inc=1, device_id=at(x, (y + d) % NY, z))
+    pl.semaphore_signal(barrier, inc=1, device_id=at(x, y, 1 - z))
+
+    def pack(xx):
+        @pl.loop(0, NY)
+        def _(k):
+            first = pl.multiple_of((xx * NY + k) * 24, 8)
+            chunk = g_ref[pl.ds(first, 24), :]
+            sx[xx, k] = jnp.concatenate([fold(chunk[0:12]), fold(chunk[12:24])], axis=0).astype(jnp.bfloat16)
+
+    vx[x] = v_ref[...]
+    started = []
+    for d in range(1, NX):
+        to = (x + d) % NX
+        pack(to)
+        if d == 1:
+            pl.semaphore_wait(barrier, NX + NY - 1)
+        started.append(pltpu.make_async_remote_copy(
+            src_ref=sx.at[to], dst_ref=rx.at[d - 1], send_sem=sem_sx.at[d - 1], recv_sem=sem_rx.at[d - 1],
+            device_id=at(to, y, z)))
+        started.append(pltpu.make_async_remote_copy(
+            src_ref=v_ref, dst_ref=vx.at[x], send_sem=sem_vsx.at[d - 1], recv_sem=sem_vrx.at[d - 1],
+            device_id=at(to, y, z)))
+        started[-2].start()
+        started[-1].start()
+    pack(x)
+    for copy in started:
+        copy.wait_recv()
+
+    vsum = (vx[0] + vx[1]) + (vx[2] + vx[3])
+    vy[y] = vsum
+
+    def sum_x(k, carry):
+        total = (sx[x, k].astype(jnp.float32) + rx[0, k].astype(jnp.float32)) + (
+            rx[1, k].astype(jnp.float32) + rx[2, k].astype(jnp.float32))
+        accx[k] = total
+        sy[k] = total.astype(jnp.bfloat16)
+        return carry
+    lax.fori_loop(0, NY, sum_x, 0)
+    second = []
+    for d in range(1, NY):
+        to = (y + d) % NY
+        second.append(pltpu.make_async_remote_copy(
+            src_ref=sy.at[to], dst_ref=ry.at[d - 1], send_sem=sem_sy.at[d - 1], recv_sem=sem_ry.at[d - 1],
+            device_id=at(x, to, z)))
+        second.append(pltpu.make_async_remote_copy(
+            src_ref=vy.at[y], dst_ref=vy.at[y], send_sem=sem_vsy.at[d - 1], recv_sem=sem_vry.at[d - 1],
+            device_id=at(x, to, z)))
+        second[-2].start()
+        second[-1].start()
+    total = accx[y]
+    for d in range(1, NY):
+        second[2 * d - 2].wait_recv()
+        total = total + ry[d - 1].astype(jnp.float32)
+    for d in range(1, NY):
+        second[2 * d - 1].wait_recv()
+    vz[0] = ((vy[0] + vy[1]) + (vy[2] + vy[3])) + ((vy[4] + vy[5]) + (vy[6] + vy[7]))
+    sz[0] = total[0:8]
+    sz[1] = total[8:16]
+    last = [
+        pltpu.make_async_remote_copy(
+            src_ref=sz.at[1 - z], dst_ref=rz, send_sem=sem_z.at[0], recv_sem=sem_z.at[1], device_id=at(x, y, 1 - z)),
+        pltpu.make_async_remote_copy(
+            src_ref=vz.at[0], dst_ref=vz.at[1], send_sem=sem_vz.at[0], recv_sem=sem_vz.at[1],
+            device_id=at(x, y, 1 - z)),
+    ]
+    for copy in last:
+        copy.start()
+    for copy in last:
+        copy.wait_recv()
+    scale = 1.0 / (NX * NY * NZ)
+    out_ref[...] = unfold((sz[z] + rz[...]) * scale)
+    vout_ref[...] = (vz[0] + vz[1]) * scale
+    for copy in started + second + last:
+        copy.wait_send()
+
+
+def reduce_grads(grad_w, vectors):
+    return pl.pallas_call(
+        reduce_kernel,
+        out_shape=(
+            jax.ShapeDtypeStruct((ROWS_DEV, D), jnp.float32),
+            jax.ShapeDtypeStruct((16, 128), jnp.float32),
+        ),
+        in_specs=[pl.BlockSpec(memory_space=pltpu.VMEM)] * 2,
+        out_specs=[pl.BlockSpec(memory_space=pltpu.VMEM)] * 2,
+        scratch_shapes=[
+            pltpu.VMEM((NX, NY, 16, FOLD), jnp.bfloat16),
+            pltpu.VMEM((NX - 1, NY, 16, FOLD), jnp.bfloat16),
+            pltpu.VMEM((NY, 16, FOLD), jnp.bfloat16),
+            pltpu.VMEM((NY - 1, 16, FOLD), jnp.bfloat16),
+            pltpu.VMEM((NY, 16, FOLD), jnp.float32),
+            pltpu.VMEM((2, 8, FOLD), jnp.float32),
+            pltpu.VMEM((8, FOLD), jnp.float32),
+            pltpu.VMEM((NX, 16, 128), jnp.float32),
+            pltpu.VMEM((NY, 16, 128), jnp.float32),
+            pltpu.VMEM((2, 16, 128), jnp.float32),
+            pltpu.SemaphoreType.DMA((NX - 1,)),
+            pltpu.SemaphoreType.DMA((NX - 1,)),
+            pltpu.SemaphoreType.DMA((NY - 1,)),
+            pltpu.SemaphoreType.DMA((NY - 1,)),
+            pltpu.SemaphoreType.DMA((2,)),
+            pltpu.SemaphoreType.DMA((NX - 1,)),
+            pltpu.SemaphoreType.DMA((NX - 1,)),
+            pltpu.SemaphoreType.DMA((NY - 1,)),
+            pltpu.SemaphoreType.DMA((NY - 1,)),
+            pltpu.SemaphoreType.DMA((2,)),
+        ],
+        compiler_params=pltpu.CompilerParams(
+            collective_id=0, has_side_effects=True, vmem_limit_bytes=32 * 1024 * 1024),
+        name="reduce_grads",
+    )(grad_w, vectors)
 
 
 def body(
@@ -39,7 +186,6 @@
     positives,
 ):
     n_enc = lax.axis_size("enc")
-    n_dp = lax.axis_size("dp")
     blocks_dev = ITEMS_DEV * BLOCKS_ITEM
     capacity = max(2, (blocks_dev + n_enc - 1) // n_enc)
     slots = n_enc * capacity
@@ -103,10 +249,10 @@
     grad_terms = jnp.einsum(
         "skrp,skrd->pd", received, d_proj_low, preferred_element_type=jnp.float32
     )
-    total_w, total_b, total_g = lax.psum((grad_terms, d_bias, d_gain), "dp")
-    row_count = PATCH_IN // n_dp
-    mine = lax.dynamic_slice_in_dim(total_w, lax.axis_index("dp") * row_count, row_count, 0)
-    return (d_user, (mine / n_dp)[None], (total_b / n_dp)[None], (total_g / n_dp)[None])
+    vectors = jnp.concatenate([d_bias, d_gain, jnp.zeros((512,), jnp.float32)]).reshape(16, 128)
+    mine, vectors = reduce_grads(grad_terms, vectors)
+    flat = vectors.reshape(-1)
+    return (d_user, mine[None], flat[None, :D], flat[None, D : 2 * D])
 
 
 def solution(mesh):

time: 1190 us -> 182 us (0.15); the launches traced: 1180 us -> 182 us
  waiting for transfers between devices: 799 us -> 74.5 us
  blocking collectives: 302 us -> 0 us
  Pallas kernels: 0 us -> 43.5 us
  between operations: 15.1 us -> 1.68 us
    psum x1 -> x0, waiting for transfers between devices: 730 us -> none  [body(): total_w, total_b, total_g = lax.psum((grad_terms, d_bias, d_gain), 'dp')]
    psum x1 -> x0, blocking collectives: 290 us -> none  [body(): total_w, total_b, total_g = lax.psum((grad_terms, d_bias, d_gain), 'dp')]
    pallas_call x0 -> x1, Pallas kernels: none -> 43.5 us  [reduce_grads(): pl.pallas_call(reduce_kernel, out_shape=(jax.ShapeDtypeStruct((ROWS_DEV,...]
  transfers between devices with their start and end apart: 3 -> 3, of which waited for: 3 -> 3; matrix products, arithmetic and copies ran while one was open for 1% -> 3% of each run, Pallas kernels for 0% -> 0%
where the time goes in v1:
time: 182 us
  waiting for transfers between devices  74.5 us (41%)
  Pallas kernels  43.5 us (24%)
  starting transfers between devices  20.4 us (11%)
  other arithmetic  16.5 us (9%)
  matrix products  12.5 us (7%)
  local copies, waits for them, and re-layouts  12.4 us (7%)
    all_to_all x1, waiting for transfers between devices, body(): lax.all_to_all(outgoing, 'enc', split_axis=0, concat_axis=0, tiled=True)  60 us
    pallas_call x1, Pallas kernels, reduce_grads(): pl.pallas_call(reduce_kernel, out_shape=(jax.ShapeDtypeStruct((ROWS_DEV,...  43.5 us
    all_to_all x1, starting transfers between devices, body(): lax.all_to_all(outgoing, 'enc', split_axis=0, concat_axis=0, tiled=True)  12.1 us
    all_to_all x1, waiting for transfers between devices, body(): lax.all_to_all(partial_value, 'enc', split_axis=0, concat_axis=0, tiled=T...  8.73 us
    reduce_sum x1, other arithmetic, pooled_rows(): normed = deviation * lax.rsqrt(variance + norm_eps) * gain_rows  5.99 us
    all_to_all x1, waiting for transfers between devices, body(): lax.all_to_all(grad_out, 'enc', split_axis=0, concat_axis=0, tiled=True)  5.8 us
    reshape x2, local copies, waits for them, and re-layouts, body(): outgoing = outgoing.reshape(n_enc, capacity, BLOCK_ROWS, PATCH_IN)  5.38 us
    reduce_sum x1, other arithmetic, pooled_rows(): deviation = shifted - center  4.87 us
  transfers between devices with their start and end apart: 3, of which 3 were waited for; matrix products, arithmetic and copies ran while one was open for 3% of the time, Pallas kernels for 0%

profile of v1, /device:TPU:6, one launch (start us, length us, event | category | flops | bytes accessed | tf_op | source)
XLA Modules:
  0.0 181.5 jit_solution(5263673905877938647)
XLA Ops:
  0.6 0.0 copy-start
  0.6 0.0 copy-start.6
  1.4 1.4 copy.28
  2.8 2.4 %reshape.134 = bf16[16,37632]{1,0:T(8,128)(2,1)} reshape(bf16[4,196,768]{2,1,0:T(8,128)(2,1)S(1)} %copy.28) | data formatting | bytes 2408448 | tf_op jit(solution)/shard_map/reshape | solution.py:193
  5.2 0.0 copy-done.6
  5.2 0.1 fusion.38
  5.3 0.2 select_reduce_fusion.1
  5.5 3.1 %convolution_convert_fusion = bf16[24,37632]{1,0:T(8,128)(2,1)} fusion(bf16[16,37632]{1,0:T(8,128)(2,1)} %reshape.134, s32[16]{0:T(128)S(1)} %select_reduce_fusion.1, pred[16]{0:T(512)(128)(4,1)S(1)} %fusion.48), kind=kOutput, calls=%fused_computation | convolution fusion | flops 29805312 | bytes 3010640 | tf_op jit(solution)/shard_map/dot_general | solution.py:202
  8.7 2.7 %reshape.135 = bf16[12,2,49,768]{3,2,1,0:T(8,128)(2,1)S(1)} reshape(bf16[24,37632]{1,0:T(8,128)(2,1)} %convolution_convert_fusion) | data formatting | bytes 3612672 | tf_op jit(solution)/shard_map/reshape | solution.py:203
  11.4 0.0 copy-start.4
  11.4 0.0 copy-start.5
  11.4 0.0 copy-start.3
  11.4 0.0 copy-start.8
  11.5 0.0 copy-start.7
  11.5 2.6 %copy.29 = bf16[12,2,49,768]{3,1,2,0:T(2,128)(2,1)} copy(bf16[12,2,49,768]{3,2,1,0:T(8,128)(2,1)S(1)} %reshape.135) | data formatting | bytes 3612672 | tf_op jit(solution)/shard_map/reshape | solution.py:203
  14.1 12.1 %all-to-all-start = ((bf16[12,2,49,768]{3,1,2,0:T(2,128)(2,1)}), bf16[12,2,49,768]{3,1,2,0:T(2,128)(2,1)S(1)}, u32[]{:S(2)}, u32[]{:S(2)}) async-start(bf16[12,2,49,768]{3,1,2,0:T(2,128)(2,1)} %copy.29), calls=%async_computation | async-start | bytes 3612672 | tf_op jit(solution)/shard_map/all_to_all | solution.py:207
  26.2 0.1 eq.79
  26.3 0.0 copy-done.4
  26.4 0.0 copy-done.5
  26.4 0.0 copy-done.3
  26.4 0.0 copy-done.8
  26.4 0.9 select_reduce_fusion
  27.3 0.0 copy-done.7
  27.3 0.1 and_select_fusion
  27.5 1.9 %convolution_convert_fusion.2 = bf16[256,768]{1,0:T(8,128)(2,1)S(1)} fusion(bf16[256,768]{1,0:T(8,128)(2,1)} %param.19, bf16[768,768]{1,0:T(8,128)(2,1)} %param.20), kind=kOutput, calls=%fused_computation.29 | convolution fusion | flops 302186496 | bytes 1966080 | tf_op jit(solution)/shard_map/dot_general | solution.py:216
  29.3 60.0 %all-to-all-done = bf16[12,2,49,768]{3,1,2,0:T(2,128)(2,1)S(1)} async-done(((bf16[12,2,49,768]{3,1,2,0:T(2,128)(2,1)}), bf16[12,2,49,768]{3,1,2,0:T(2,128)(2,1)S(1)}, u32[]{:S(2)}, u32[]{:S(2)}) %all-to-all-start) | async-done | bytes 1806368 | tf_op jit(solution)/shard_map/all_to_all | solution.py:207
  89.3 0.0 copy-done
  89.4 1.9 %add_reduce_fusion.1 = (f32[12,2,49]{2,1,0:T(2,128)S(1)}, f32[12,2,49,768]{3,2,1,0:T(8,128)S(1)}) fusion(f32[768]{0:T(1024)S(1)} %reduce, bf16[1,768,768]{2,1,0:T(8,128)(2,1)S(1)} %copy-done, bf16[12,2,49,768]{3,1,2,0:T(2,128)(2,1)S(1)} %all-to-all-done), kind=kOutput, calls=%fused_computation.20 | convolution fusion | flops 1389071232 | bytes 6606432 | tf_op jit(solution)/shard_map/skrp,pd->skrd/dot_general | solution.py:208
  91.3 0.0 copy-start.1
  91.3 0.8 multiply_reduce_fusion.2
  92.1 1.1 copy-done.1
  93.2 2.9 %fusion.7 = bf16[12,2,768]{2,1,0:T(2,128)(2,1)} fusion(f32[768]{0:T(1024)S(1)} %reduce.1, f32[12,2,49]{2,1,0:T(2,128)S(1)} %fusion.39, f32[12,2,49]{2,1,0:T(2,128)S(1)} %broadcast_multiply_fusion, f32[12,2,49,768]{3,2,1,0:T(8,128)S(1)} %get-tuple-element.35, f32[768]{0:T(1024)S(1)} %reduce), kind=kLoop, calls=%fused_computation.14 | loop fusion | flops 11722752 | bytes 3665088 | tf_op jit(solution)/shard_map/jvp()/reduce_sum | solution.py:31
  96.2 4.6 %all-to-all-start.1 = ((bf16[12,2,768]{2,1,0:T(2,128)(2,1)}), bf16[12,2,768]{2,1,0:T(2,128)(2,1)S(1)}, u32[]{:S(2)}, u32[]{:S(2)}) async-start(bf16[12,2,768]{2,1,0:T(2,128)(2,1)} %fusion.7), calls=%async_computation.1 | async-start | bytes 73728 | tf_op jit(solution)/shard_map/all_to_all | solution.py:212
  100.8 8.7 %all-to-all-done.1 = bf16[12,2,768]{2,1,0:T(2,128)(2,1)S(1)} async-done(((bf16[12,2,768]{2,1,0:T(2,128)(2,1)}), bf16[12,2,768]{2,1,0:T(2,128)(2,1)S(1)}, u32[]{:S(2)}, u32[]{:S(2)}) %all-to-all-start.1) | async-done | bytes 36896 | tf_op jit(solution)/shard_map/all_to_all | solution.py:212
  109.6 0.2 convolution_reduce_fusion
  109.8 0.3 fusion.29
  110.1 0.2 fusion.20
  110.3 0.1 convolution_convert_fusion.3
  110.4 0.6 reshape.138
  111.1 3.7 %all-to-all-start.2 = ((bf16[12,2,768]{2,1,0:T(2,128)(2,1)}), bf16[12,2,768]{2,1,0:T(2,128)(2,1)S(1)}, u32[]{:S(2)}, u32[]{:S(2)}) async-start(bf16[12,2,768]{2,1,0:T(2,128)(2,1)} %reshape.138), calls=%async_computation.2 | async-start | bytes 73728 | tf_op jit(solution)/shard_map/all_to_all | solution.py:245
  114.7 2.7 %convolution_convert_fusion.1 = bf16[256,768]{1,0:T(8,128)(2,1)} fusion(bf16[768,768]{1,0:T(8,128)(2,1)} %param.20, bf16[256,4]{0,1:T(4,128)(2,1)S(1)} %fusion.29, f32[4,768]{1,0:T(4,128)S(1)} %convolution_reduce_fusion), kind=kOutput, calls=%fused_computation.28 | convolution fusion | flops 304158720 | bytes 1587200 | tf_op jit(solution)/shard_map/dot_general | solution.py:239
  117.4 5.8 %all-to-all-done.2 = bf16[12,2,768]{2,1,0:T(2,128)(2,1)S(1)} async-done(((bf16[12,2,768]{2,1,0:T(2,128)(2,1)}), bf16[12,2,768]{2,1,0:T(2,128)(2,1)S(1)}, u32[]{:S(2)}, u32[]{:S(2)}) %all-to-all-start.2) | async-done | bytes 36896 | tf_op jit(solution)/shard_map/all_to_all | solution.py:245
  123.2 0.0 copy-start.2
  123.2 0.1 convert_multiply_fusion.1
  123.3 6.0 %multiply_reduce_fusion = (f32[768]{0:T(1024)S(1)}, f32[12,2,49]{2,1,0:T(2,128)S(1)}) fusion(f32[12,2,49]{2,1,0:T(2,128)S(1)} %fusion.39, f32[12,2,49]{2,1,0:T(2,128)S(1)} %broadcast_multiply_fusion, f32[12,2,49,768]{3,2,1,0:T(8,128)} %copy-done.1, f32[768]{0:T(1024)S(1)} %reduce, f32[12,2,768]{2,1,0:T(2,128)S(1)} %get-tuple-element.31, ...), kind=kLoop, calls=%fused_computation.10 | loop fusion | flops 24383592 | bytes 3783456 | tf_op jit(solution)/shard_map/transpose(jvp())/reduce_sum | solution.py:30
  129.3 0.0 copy-done.2
  129.3 4.9 %fusion.53 = (f32[12,2,49]{2,1,0:T(2,128)S(1)}, f32[12,2,49,768]{3,2,1,0:T(8,128)S(1)}) fusion(f32[12,2,49]{2,1,0:T(2,128)S(1)} %multiply_multiply_fusion.3, f32[12,2,768]{2,1,0:T(2,128)S(1)} %get-tuple-element.31, f32[12,2,768]{2,1,0:T(2,128)S(1)} %get-tuple-element.30, f32[768]{0:T(1024)S(1)} %reduce.1, f32[12,2,49]{2,1,0:T(2,128)S(1)} %fusion.39, ...), kind=kLoop, calls=%fused_computation.95 | loop fusion | flops 25287528 | bytes 7397760 | tf_op jit(solution)/shard_map/transpose(jvp())/reduce_sum | solution.py:28
  134.2 0.5 add_reduce_fusion
  134.7 2.1 %fusion.13.g_ref = f32[768,768]{1,0:T(8,128)S(1)} fusion(bf16[12,2,49,768]{3,2,1,0:T(8,128)(2,1)S(1)} %get-tuple-element.29, bf16[12,2,49,768]{3,1,2,0:T(2,128)(2,1)S(1)} %all-to-all-done), kind=kOutput, calls=%fused_computation.26 | convolution fusion | flops 1387266048 | bytes 5971968 | tf_op jit(solution)/shard_map/skrp,skrd->pd/dot_general | solution.py:249
  136.8 43.5 %reduce_grads.1 = (f32[12,768]{1,0:T(8,128)S(1)}, f32[16,128]{1,0:T(8,128)S(1)}) custom-call(f32[768,768]{1,0:T(8,128)S(1)} %fusion.13.g_ref, f32[16,128]{1,0:T(8,128)S(1)} %maximum_bitcast_fusion.v_ref), custom_call_target="tpu_custom_call" | custom-call | tf_op jit(solution)/shard_map/reduce_grads/pallas_call | solution.py:139
  180.3 0.7 copy.33
  180.9 0.6 copy_bitcast_fusion
  (17 shorter events, 0.2 us)
Async XLA Ops:
  0.6 88.7 %copy-start = (bf16[1,768,768]{2,1,0:T(8,128)(2,1)S(1)}, bf16[1,768,768]{2,1,0:T(8,128)(2,1)}, u32[]{:S(2)}) copy-start(bf16[1,768,768]{2,1,0:T(8,128)(2,1)} %param.15) | copy-start | bytes 3538948
  0.6 4.6 %copy-start.6 = (s32[16]{0:T(128)S(1)}, s32[16]{0:T(128)}, u32[]{:S(2)}) copy-start(s32[16]{0:T(128)} %param.14) | copy-start | bytes 196
  11.4 14.9 %copy-start.4 = (f32[1,768]{1,0:T(1,128)S(1)}, f32[1,768]{1,0:T(1,128)}, u32[]{:S(2)}) copy-start(f32[1,768]{1,0:T(1,128)} %param.16) | copy-start | bytes 9220
  11.4 14.9 %copy-start.5 = (f32[1,768]{1,0:T(1,128)S(1)}, f32[1,768]{1,0:T(1,128)}, u32[]{:S(2)}) copy-start(f32[1,768]{1,0:T(1,128)} %param.17) | copy-start | bytes 9220
  11.4 15.0 %copy-start.3 = (f32[65536]{0:T(1024)S(1)}, f32[65536]{0:T(1024)}, u32[]{:S(2)}) copy-start(f32[65536]{0:T(1024)} %param.18) | copy-start | bytes 786436
  11.4 15.0 %copy-start.8 = (s32[4]{0:T(128)S(1)}, s32[4]{0:T(128)}, u32[]{:S(2)}) copy-start(s32[4]{0:T(128)} %param.13) | copy-start | bytes 52
  11.5 15.9 %copy-start.7 = (s32[256]{0:T(256)S(1)}, s32[256]{0:T(256)}, u32[]{:S(2)}) copy-start(s32[256]{0:T(256)} %param.21) | copy-start | bytes 3076
  14.1 75.2 %all-to-all-start = ((bf16[12,2,49,768]{3,1,2,0:T(2,128)(2,1)}), bf16[12,2,49,768]{3,1,2,0:T(2,128)(2,1)S(1)}, u32[]{:S(2)}, u32[]{:S(2)}) async-start(bf16[12,2,49,768]{3,1,2,0:T(2,128)(2,1)} %copy.29), calls=%async_computation | async-start | bytes 3612672 | tf_op jit(solution)/shard_map/all_to_all | solution.py:207
  91.3 1.9 %copy-start.1 = (f32[12,2,49,768]{3,2,1,0:T(8,128)}, f32[12,2,49,768]{3,2,1,0:T(8,128)S(1)}, u32[]{:S(2)}) copy-start(f32[12,2,49,768]{3,2,1,0:T(8,128)S(1)} %get-tuple-element.35) | copy-start | bytes 10838020
  96.2 13.4 %all-to-all-start.1 = ((bf16[12,2,768]{2,1,0:T(2,128)(2,1)}), bf16[12,2,768]{2,1,0:T(2,128)(2,1)S(1)}, u32[]{:S(2)}, u32[]{:S(2)}) async-start(bf16[12,2,768]{2,1,0:T(2,128)(2,1)} %fusion.7), calls=%async_computation.1 | async-start | bytes 73728 | tf_op jit(solution)/shard_map/all_to_all | solution.py:212
  111.1 12.2 %all-to-all-start.2 = ((bf16[12,2,768]{2,1,0:T(2,128)(2,1)}), bf16[12,2,768]{2,1,0:T(2,128)(2,1)S(1)}, u32[]{:S(2)}, u32[]{:S(2)}) async-start(bf16[12,2,768]{2,1,0:T(2,128)(2,1)} %reshape.138), calls=%async_computation.2 | async-start | bytes 73728 | tf_op jit(solution)/shard_map/all_to_all | solution.py:245
  123.2 6.1 %copy-start.2 = (f32[12,2,49,768]{3,2,1,0:T(8,128)S(1)}, f32[12,2,49,768]{3,2,1,0:T(8,128)}, u32[]{:S(2)}) copy-start(f32[12,2,49,768]{3,2,1,0:T(8,128)} %copy-done.1) | copy-start | bytes 10838020

commit v2 on v0

v2 whole, which is shorter than its diff:
```python
import jax
import jax.numpy as jnp
from jax import lax
from jax.experimental import pallas as pl
from jax.experimental.pallas import tpu as pltpu
from jax.sharding import PartitionSpec as P

D = 768
PATCHES = 196
BLOCK_ROWS = 49
BLOCKS_ITEM = 4
ITEMS_DEV = 4
BLOCKS_DEV = ITEMS_DEV * BLOCKS_ITEM
USERS_DEV = 256
CAP = 2
N_ENC = 12
SLOTS = N_ENC * CAP
MAIN = 48
NX, NY, NZ = 4, 8, 2
ROWS_DEV = 12
FOLD = 1152
LANES = 128
PIECES = D // LANES
GROUP = 16

score_scale = 0.1
loss_weight = 16.0
norm_eps = 1e-05
GELU_A = 0.7978845608028654
GELU_B = 0.044715

f32 = jnp.float32
bf16 = jnp.bfloat16


def fold(rows):
    tail = rows[8:12]
    return jnp.concatenate([rows[0:8], jnp.concatenate([tail[:, :384], tail[:, 384:]], axis=0)], axis=1)


def unfold(folded):
    tail = folded[:, 768:]
    return jnp.concatenate([folded[:, :768], jnp.concatenate([tail[0:4], tail[4:8]], axis=1)], axis=0)


def row_to_tile(row):
    pieces = [row[:, c * LANES : (c + 1) * LANES] for c in range(PIECES)]
    return jnp.concatenate(pieces + [jnp.zeros((2, LANES), row.dtype)], axis=0)


def tile_to_row(tile):
    return jnp.concatenate([tile[c : c + 1] for c in range(PIECES)], axis=1)


def sign3(core):
    return 1 - 2 * core


def offset(p, core):
    return ((p + 1) // 2) * (2 * (p % 2) - 1) * (1 + (p // 5) * (sign3(core) - 1))


def normed_rows(projected, bias, gain):
    shifted = projected + bias
    center = jnp.sum(shifted, axis=-1, keepdims=True) * (1.0 / D)
    deviation = shifted - center
    variance = jnp.sum(deviation * deviation, axis=-1, keepdims=True) * (1.0 / D)
    rstd = lax.rsqrt(variance + norm_eps)
    xhat = deviation * rstd
    n = xhat * gain
    square = n * n
    t = jnp.tanh(n * (GELU_A + (GELU_A * GELU_B) * square))
    half = 0.5 + 0.5 * t
    act = n * half
    slope = half + (0.5 * n) * (1.0 - t * t) * (GELU_A + (3.0 * GELU_A * GELU_B) * square)
    return act, slope, xhat, rstd


def rows_back(u, slope, xhat, rstd):
    t = slope * u
    m1 = jnp.sum(t, axis=-1, keepdims=True) * (1.0 / D)
    m2 = jnp.sum(t * xhat, axis=-1, keepdims=True) * (1.0 / D)
    return rstd * (t - m1 - xhat * m2)


def step_kernel(
    src_ref, ids_ref, live_ref, items_ref, chosen_ref, patches_ref, w_ref, bias_ref, gain_ref, ibias_ref,
    users_ref, proj_ref,
    duser_ref, out_ref, bout_ref, gout_ref,
    main, tails, send, recv, tsend, trecv, trows, xtail, psend, precv, dsend, drecv,
    proj, xhat_m, slope_m, rstd_m, act_t, xhat_t, slope_t, rstd_t, dtail, gsum, dlow, dlow_t, uvec, dbacc, g,
    sx, rx, sy, ry, accx, sz, rz, vown, vx, vy, vz,
    sem_s, sem_r, sem_ts, sem_tr, sem_ps, sem_pr, sem_ds, sem_dr,
    sem_sx, sem_rx, sem_sy, sem_ry, sem_z, sem_vsx, sem_vrx, sem_vsy, sem_vry, sem_vz,
):
    dp = lax.axis_index("dp")
    enc = lax.axis_index("enc")
    x = dp // (NY * NZ)
    y = (dp // NZ) % NY
    z = dp % NZ
    core = enc % 2
    ring = z * 6 + enc // 2

    def at(xx, yy, zz):
        return {"dp": (xx * NY + yy) * NZ + zz}

    def on_ring(place, which):
        place = (place + 12) % 12
        return {"dp": (x * NY + y) * NZ + place // 6, "enc": (place % 6) * 2 + which}

    def dest(p, r):
        return on_ring(ring + offset(p, core), (core + r) % 2)

    def source(p, r):
        other = (core + r) % 2
        return on_ring(ring - offset(p, other), other)

    barrier = pltpu.get_barrier_semaphore()
    partners = 0
    for p in range(6):
        for r in range(2):
            if p or r:
                pl.semaphore_signal(barrier, inc=1, device_id=source(p, r))
                partners += 1
    for d in range(1, NX):
        pl.semaphore_signal(barrier, inc=1, device_id=at((x + d) % NX, y, z))
    for d in range(1, NY):
        pl.semaphore_signal(barrier, inc=1, device_id=at(x, (y + d) % NY, z))
    pl.semaphore_signal(barrier, inc=1, device_id=at(x, y, 1 - z))
    partners += NX + NY - 1

    tails[...] = jnp.zeros_like(tails)
    row = lax.broadcasted_iota(jnp.int32, (208, PATCHES), 0)
    col = lax.broadcasted_iota(jnp.int32, (208, PATCHES), 1)
    steps = (row >= 48).astype(jnp.int32) + (row >= 96).astype(jnp.int32) + (row >= 144).astype(jnp.int32)
    origin = jnp.where(row < 192, row + steps, (row - 192) * BLOCK_ROWS + MAIN)
    order = jnp.where(origin == col, 1.0, 0.0).astype(bf16)
    for i in range(ITEMS_DEV):
        sorted_rows = jnp.dot(order, patches_ref[i], preferred_element_type=f32)
        for b in range(BLOCKS_ITEM):
            main[i * BLOCKS_ITEM + b] = sorted_rows[b * MAIN : (b + 1) * MAIN].astype(bf16)
            tails[i * BLOCKS_ITEM + b] = row_to_tile(sorted_rows[192 + b : 193 + b])

    def remote(src, dst, ssem, rsem, device):
        return pltpu.make_async_remote_copy(
            src_ref=src, dst_ref=dst, send_sem=ssem, recv_sem=rsem, device_id=device)

    def tail_tile(j):
        return jnp.concatenate([tails[src_ref[2 * j]], tails[src_ref[2 * j + 1]]], axis=0).astype(bf16)

    trecv[0] = tail_tile(0)
    for j in range(1, N_ENC):
        tsend[j] = tail_tile(j)
    pl.semaphore_wait(barrier, partners)
    started = []

    def start(copy):
        copy.start()
        started.append(copy)
        return copy

    for j in range(1, N_ENC):
        start(remote(tsend.at[j], trecv.at[j], sem_ts.at[j], sem_tr.at[j], dest(j // 2, j % 2)))
    for p in (5, 4, 3, 2, 1, 0):
        for r in range(2):
            j = 2 * p + r
            if j:
                for k in range(CAP):
                    send[j, k] = main[src_ref[2 * j + k]]
                start(remote(send.at[j], recv.at[j], sem_s.at[j], sem_r.at[j], dest(p, r)))
    for k in range(CAP):
        recv[0, k] = main[src_ref[k]]

    @pl.loop(0, D // 256)
    def _(m):
        first = pl.multiple_of(m * 256, 256)
        uvec[:, pl.ds(first, 256)] = jnp.dot(
            users_ref[...], proj_ref[:, pl.ds(first, 256)], preferred_element_type=f32).astype(bf16)

    entry = lax.broadcasted_iota(jnp.int32, (512, LANES), 0) * LANES + lax.broadcasted_iota(jnp.int32, (512, LANES), 1)
    item_row = lax.broadcasted_iota(jnp.int32, (8, 1), 0)
    item_biases = jnp.zeros((8, 1), f32)
    for i in range(ITEMS_DEV):
        picked = jnp.where(entry == ids_ref[i], ibias_ref[...], 0.0)
        picked = jnp.sum(jnp.sum(picked, axis=0, keepdims=True), axis=1, keepdims=True)
        item_biases = item_biases + jnp.where(item_row == i, picked, 0.0)

    out_row = lax.broadcasted_iota(jnp.int32, (48, N_ENC * 16), 0)
    in_col = lax.broadcasted_iota(jnp.int32, (48, N_ENC * 16), 1)
    belongs = ((out_row & 7) == items_ref[...]) & ((out_row >> 3) == (in_col & 7))
    belongs = jnp.where(belongs, 1.0, 0.0).astype(bf16)

    bias = bias_ref[...]
    gain = gain_ref[...]

    trows[...] = jnp.zeros_like(trows)
    for j in range(N_ENC):
        if j:
            remote(tsend.at[j], trecv.at[j], sem_ts.at[j], sem_tr.at[j], dest(j // 2, j % 2)).wait_recv()
        tile = trecv[j].astype(f32)
        for k in range(CAP):
            trows[2 * j + k : 2 * j + k + 1, :] = tile_to_row(tile[8 * k : 8 * k + 8])
    xtail[...] = trows[...].astype(bf16)
    proj[0:32, :] = jnp.dot(xtail[...], w_ref[...], preferred_element_type=f32)
    for s in range(2):
        rows = slice(s * GROUP, (s + 1) * GROUP)
        act, slope, xhat, rstd = normed_rows(proj[rows, :], bias, gain)
        act_t[rows, :] = act
        slope_t[rows, :] = slope
        xhat_t[rows, :] = xhat
        rstd_t[rows, :] = jnp.broadcast_to(rstd, (GROUP, LANES))

    def forward(q, carry):
        p = (6 - q) % 6
        for r in range(2):
            @pl.when(2 * p + r > 0)
            def _():
                remote(send.at[2 * p + r], recv.at[2 * p + r], sem_s.at[2 * p + r], sem_r.at[2 * p + r],
                       {"enc": (enc // 2) * 2 + 1 - core}).wait_recv()
        @pl.loop(0, D // 256)
        def _(m):
            first = pl.multiple_of(m * 256, 256)
            proj[:, pl.ds(first, 256)] = jnp.dot(
                recv[pl.ds(2 * p, 2)].reshape(4 * MAIN, D), w_ref[:, pl.ds(first, 256)], preferred_element_type=f32)

        def slot(s, carry):
            own = 4 * p + s
            pooled = act_t[pl.ds(own, 1), :]
            weighted = slope_t[pl.ds(own, 1), :] * xhat_t[pl.ds(own, 1), :]
            pool, gs = None, None
            for m in range(MAIN // GROUP):
                act, slope, xhat, rstd = normed_rows(
                    proj[pl.ds(pl.multiple_of(s * MAIN + m * GROUP, GROUP), GROUP), :], bias, gain)
                rows = slice(m * GROUP, (m + 1) * GROUP)
                slope_m[own, rows, :] = slope
                xhat_m[own, rows, :] = xhat
                rstd_m[own, rows, :] = jnp.broadcast_to(rstd, (GROUP, LANES))
                product = slope * xhat
                act = act[0:8] + act[8:16]
                product = product[0:8] + product[8:16]
                pool = act if pool is None else pool + act
                gs = product if gs is None else gs + product
            gsum[pl.ds(own, 1), :] = jnp.sum(gs, axis=0, keepdims=True) + weighted
            trows[pl.ds(own, 1), :] = jnp.sum(pool, axis=0, keepdims=True) + pooled
            return carry
        lax.fori_loop(0, 4, slot, 0)
        for r in range(2):
            j = 2 * p + r
            tile = jnp.concatenate(
                [row_to_tile(trows[pl.ds(2 * j + k, 1), :]) for k in range(CAP)], axis=0).astype(bf16)
            psend[j] = tile
            if r == 0:
                @pl.when(p == 0)
                def _():
                    precv[0] = tile

            @pl.when(j > 0)
            def _():
                remote(psend.at[j], precv.at[j], sem_ps.at[j], sem_pr.at[j], source(p, r)).start()
        return carry
    lax.fori_loop(0, 6, forward, 0)

    returned = [remote(psend.at[j], precv.at[j], sem_ps.at[j], sem_pr.at[j], source(j // 2, j % 2)) for j in range(1, N_ENC)]
    for copy in returned:
        copy.wait_recv()
    summed = jnp.dot(belongs, precv[...].reshape(N_ENC * 16, LANES), preferred_element_type=f32)
    embed = jnp.concatenate([summed[8 * c : 8 * c + 8] for c in range(PIECES)], axis=1)
    embed = (embed / PATCHES).astype(bf16)
    scores = lax.dot_general(embed, uvec[...], (((1,), (1,)), ((), ())), preferred_element_type=f32)
    scores = scores * score_scale + item_biases
    index = lax.broadcasted_iota(jnp.int32, (8, USERS_DEV), 0)
    target = jnp.where(index == chosen_ref[...], 1.0, 0.0)
    sigmoid = 1.0 / (1.0 + jnp.exp(-scores))
    d_score = jnp.where(index < live_ref[0], loss_weight * (sigmoid - target), 0.0).astype(bf16)
    d_embed = jnp.dot(d_score, uvec[...], preferred_element_type=f32) * score_scale
    d_folded = jnp.concatenate([d_embed[:, c * LANES : (c + 1) * LANES] for c in range(PIECES)], axis=0).astype(bf16)
    d_slots = lax.dot_general(belongs, d_folded, (((0,), (0,)), ((), ())), preferred_element_type=f32)
    dsend[...] = d_slots.astype(bf16).reshape(N_ENC, 16, LANES)
    for p in (5, 4, 3, 2, 1, 0):
        for r in range(2):
            j = 2 * p + r
            if j:
                start(remote(dsend.at[j], drecv.at[j], sem_ds.at[j], sem_dr.at[j], dest(p, r)))
    drecv[0] = dsend[0]
    d_user_vec = lax.dot_general(d_score, embed, (((0,), (0,)), ((), ())), preferred_element_type=f32)
    uvec[...] = (d_user_vec * score_scale).astype(bf16)

    @pl.loop(0, D // 256)
    def _(m):
        first = pl.multiple_of(m * 256, 256)
        duser_ref[:, pl.ds(first, 256)] = lax.dot_general(
            uvec[...], proj_ref[pl.ds(first, 256), :], (((1,), (1,)), ((), ())), preferred_element_type=f32).astype(bf16)

    dtail[...] = jnp.zeros_like(dtail)
    dbacc[...] = jnp.zeros_like(dbacc)

    def backward(j, carry):
        @pl.when(j > 0)
        def _():
            remote(dsend.at[j], drecv.at[j], sem_ds.at[j], sem_dr.at[j],
                   {"enc": (enc // 2) * 2 + 1 - core}).wait_recv()
        tile = drecv[j].astype(f32) / PATCHES
        for k in range(CAP):
            own = 2 * j + k
            d_row = tile_to_row(tile[8 * k : 8 * k + 8])
            dtail[pl.ds(own, 1), :] = d_row
            u = d_row * gain
            for m in range(MAIN // GROUP):
                rows = slice(m * GROUP, (m + 1) * GROUP)
                rstd = jnp.concatenate([rstd_m[own, rows, :]] * PIECES, axis=1)
                d_projected = rows_back(u, slope_m[own, rows, :], xhat_m[own, rows, :], rstd)
                dlow[own, rows, :] = d_projected.astype(bf16)
                dbacc[...] += d_projected[0:8] + d_projected[8:16]
        return carry
    lax.fori_loop(0, N_ENC, backward, 0)
    for s in range(2):
        rows = slice(s * GROUP, (s + 1) * GROUP)
        rstd = jnp.concatenate([rstd_t[rows, :]] * PIECES, axis=1)
        d_projected = rows_back(dtail[rows, :] * gain, slope_t[rows, :], xhat_t[rows, :], rstd)
        dlow_t[rows, :] = d_projected.astype(bf16)
        dbacc[...] += d_projected[0:8] + d_projected[8:16]
    d_bias = jnp.sum(dbacc[...], axis=0, keepdims=True)
    d_gain = jnp.sum(dtail[0:SLOTS, :] * gsum[0:SLOTS, :], axis=0, keepdims=True)
    vectors = jnp.concatenate([row_to_tile(d_bias), row_to_tile(d_gain)], axis=0)

    @pl.loop(0, D // 256)
    def _(m):
        first = pl.multiple_of(m * 256, 256)
        g[pl.ds(first, 256), :] = lax.dot_general(
            recv[:, :, :, pl.ds(first, 256)].reshape(SLOTS * MAIN, 256), dlow[...].reshape(SLOTS * MAIN, D),
            (((0,), (0,)), ((), ())), preferred_element_type=f32) + lax.dot_general(
            xtail[:, pl.ds(first, 256)], dlow_t[...], (((0,), (0,)), ((), ())), preferred_element_type=f32)

    for copy in started + returned:
        copy.wait_send()

    vown[...] = vectors

    def pack(xx):
        @pl.loop(0, NY)
        def _(k):
            first = pl.multiple_of((xx * NY + k) * 24, 8)
            chunk = g[pl.ds(first, 24), :]
            sx[xx, k] = jnp.concatenate([fold(chunk[0:12]), fold(chunk[12:24])], axis=0).astype(bf16)

    vx[x] = vectors
    firsts = []
    for d in range(1, NX):
        to = (x + d) % NX
        pack(to)
        firsts.append(remote(sx.at[to], rx.at[d - 1], sem_sx.at[d - 1], sem_rx.at[d - 1], at(to, y, z)))
        firsts.append(remote(vown, vx.at[x], sem_vsx.at[d - 1], sem_vrx.at[d - 1], at(to, y, z)))
        firsts[-2].start()
        firsts[-1].start()
    pack(x)
    for copy in firsts:
        copy.wait_recv()
    vy[y] = (vx[0] + vx[1]) + (vx[2] + vx[3])

    def sum_x(k, carry):
        total = (sx[x, k].astype(f32) + rx[0, k].astype(f32)) + (rx[1, k].astype(f32) + rx[2, k].astype(f32))
        accx[k] = total
        sy[k] = total.astype(bf16)
        return carry
    lax.fori_loop(0, NY, sum_x, 0)
    second = []
    for d in range(1, NY):
        to = (y + d) % NY
        second.append(remote(sy.at[to], ry.at[d - 1], sem_sy.at[d - 1], sem_ry.at[d - 1], at(x, to, z)))
        second.append(remote(vy.at[y], vy.at[y], sem_vsy.at[d - 1], sem_vry.at[d - 1], at(x, to, z)))
        second[-2].start()
        second[-1].start()
    total = accx[y]
    for d in range(1, NY):
        second[2 * d - 2].wait_recv()
        total = total + ry[d - 1].astype(f32)
    for d in range(1, NY):
        second[2 * d - 1].wait_recv()
    vz[0] = ((vy[0] + vy[1]) + (vy[2] + vy[3])) + ((vy[4] + vy[5]) + (vy[6] + vy[7]))
    sz[0] = total[0:8]
    sz[1] = total[8:16]
    last = [
        remote(sz.at[1 - z], rz, sem_z.at[0], sem_z.at[1], at(x, y, 1 - z)),
        remote(vz.at[0], vz.at[1], sem_vz.at[0], sem_vz.at[1], at(x, y, 1 - z)),
    ]
    for copy in last:
        copy.start()
    for copy in last:
        copy.wait_recv()
    scale = 1.0 / (NX * NY * NZ)
    out_ref[...] = unfold((sz[z] + rz[...]) * scale)
    folded = (vz[0] + vz[1]) * scale
    bout_ref[...] = tile_to_row(folded[0:8])
    gout_ref[...] = tile_to_row(folded[8:16])
    for copy in firsts + second + last:
        copy.wait_send()


def train_step(src, ids, live, items, chosen, patches, weight, bias, gain, item_bias, users, proj):
    vmem = pl.BlockSpec(memory_space=pltpu.VMEM)
    smem = pl.BlockSpec(memory_space=pltpu.SMEM)
    dma = pltpu.SemaphoreType.DMA
    return pl.pallas_call(
        step_kernel,
        out_shape=(
            jax.ShapeDtypeStruct((USERS_DEV, D), bf16),
            jax.ShapeDtypeStruct((ROWS_DEV, D), f32),
            jax.ShapeDtypeStruct((1, D), f32),
            jax.ShapeDtypeStruct((1, D), f32),
        ),
        in_specs=[smem] * 3 + [vmem] * 9,
        out_specs=[vmem] * 4,
        scratch_shapes=[
            pltpu.VMEM((BLOCKS_DEV, MAIN, D), bf16),
            pltpu.VMEM((BLOCKS_DEV, 8, LANES), f32),
            pltpu.VMEM((N_ENC, CAP, MAIN, D), bf16),
            pltpu.VMEM((N_ENC, CAP, MAIN, D), bf16),
        ] + [pltpu.VMEM((N_ENC, 16, LANES), bf16)] * 2 + [
            pltpu.VMEM((32, D), f32),
            pltpu.VMEM((32, D), bf16),
        ] + [pltpu.VMEM((N_ENC, 16, LANES), bf16)] * 4 + [
            pltpu.VMEM((4 * MAIN, D), f32),
            pltpu.VMEM((SLOTS, MAIN, D), f32),
            pltpu.VMEM((SLOTS, MAIN, D), f32),
            pltpu.VMEM((SLOTS, MAIN, LANES), f32),
            pltpu.VMEM((32, D), f32),
            pltpu.VMEM((32, D), f32),
            pltpu.VMEM((32, D), f32),
            pltpu.VMEM((32, LANES), f32),
            pltpu.VMEM((32, D), f32),
            pltpu.VMEM((32, D), f32),
            pltpu.VMEM((SLOTS, MAIN, D), bf16),
            pltpu.VMEM((32, D), bf16),
            pltpu.VMEM((USERS_DEV, D), bf16),
            pltpu.VMEM((8, D), f32),
            pltpu.VMEM((D, D), f32),
            pltpu.VMEM((NX, NY, 16, FOLD), bf16),
            pltpu.VMEM((NX - 1, NY, 16, FOLD), bf16),
            pltpu.VMEM((NY, 16, FOLD), bf16),
            pltpu.VMEM((NY - 1, 16, FOLD), bf16),
            pltpu.VMEM((NY, 16, FOLD), f32),
            pltpu.VMEM((2, 8, FOLD), f32),
            pltpu.VMEM((8, FOLD), f32),
            pltpu.VMEM((16, LANES), f32),
            pltpu.VMEM((NX, 16, LANES), f32),
            pltpu.VMEM((NY, 16, LANES), f32),
            pltpu.VMEM((2, 16, LANES), f32),
        ] + [dma((N_ENC,))] * 8 + [
            dma((NX - 1,)), dma((NX - 1,)), dma((NY - 1,)), dma((NY - 1,)), dma((2,)),
            dma((NX - 1,)), dma((NX - 1,)), dma((NY - 1,)), dma((NY - 1,)), dma((2,)),
        ],
        compiler_params=pltpu.CompilerParams(
            collective_id=0, has_side_effects=True, vmem_limit_bytes=48 * 1024 * 1024),
        name="train_step",
    )(src, ids, live, items, chosen, patches, weight, bias, gain, item_bias, users, proj)


def body(
    patches,
    item_counts,
    item_ids,
    block_dest,
    enc_weight,
    enc_bias,
    enc_gain,
    item_bias,
    user_state,
    user_proj,
    positives,
):
    enc = lax.axis_index("enc")
    core = enc % 2
    live_items = item_counts[0]
    place = jnp.arange(N_ENC, dtype=jnp.int32)
    chip = (enc // 2 + offset(place // 2, core) + 6) % 6
    expert = chip * 2 + (core + place % 2) % 2
    number = jnp.arange(BLOCKS_DEV, dtype=jnp.int32)
    live_block = number // BLOCKS_ITEM < live_items
    routed = (block_dest[None, :] == expert[:, None]) & live_block[None, :]
    earlier = (block_dest[None, :] == block_dest[:, None]) & (number[None, :] < number[:, None])
    second = jnp.any(earlier, axis=1)
    taken = jnp.stack([routed & ~second[None, :], routed & second[None, :]], axis=1).astype(jnp.int32)
    src = jnp.sum(taken * number[None, None, :], axis=2).reshape(-1)
    present = jnp.sum(taken, axis=2).reshape(-1)
    item = jnp.where(present > 0, src // BLOCKS_ITEM, -1)
    items = jnp.broadcast_to(item[:, None], (SLOTS, 8)).reshape(1, SLOTS * 8)
    chosen = (positives % live_items)[None, :]
    d_user, mine, d_bias, d_gain = train_step(
        src, item_ids, item_counts, items, chosen, patches, enc_weight[0], enc_bias, enc_gain,
        item_bias.reshape(-1, LANES), user_state, user_proj)
    return (d_user, mine[None], d_bias, d_gain)


def solution(mesh):
    return jax.shard_map(
        body,
        mesh=mesh,
        in_specs=(
            P(("dp", "enc"), None, None),
            P(("dp", "enc")),
            P(("dp", "enc")),
            P(("dp", "enc")),
            P("enc", None, None),
            P("enc", None),
            P("enc", None),
            P(),
            P(("dp", "enc"), None),
            P(),
            P(("dp", "enc")),
        ),
        out_specs=(P(("dp", "enc"), None), P("enc", "dp", None), P("enc", None), P("enc", None)),
        check_vma=False,
    )
```

time: 1190 us -> 109 us (0.09); the launches traced: 1180 us -> 109 us
  waiting for transfers between devices: 799 us -> 0 us
  blocking collectives: 302 us -> 0 us
  Pallas kernels: 0 us -> 97.7 us
  starting transfers between devices: 16.8 us -> 0 us
  other arithmetic: 17.3 us -> 3.01 us
  matrix products: 13.9 us -> 0 us
  between operations: 15.1 us -> 1.42 us
    psum x1 -> x0, waiting for transfers between devices: 730 us -> none  [body(): total_w, total_b, total_g = lax.psum((grad_terms, d_bias, d_gain), 'dp')]
    psum x1 -> x0, blocking collectives: 290 us -> none  [body(): total_w, total_b, total_g = lax.psum((grad_terms, d_bias, d_gain), 'dp')]
    pallas_call x0 -> x1, Pallas kernels: none -> 97.7 us  [train_step(): pl.pallas_call(step_kernel, out_shape=(jax.ShapeDtypeStruct((USERS_DEV, D...]
    all_to_all x2 -> x0, waiting for transfers between devices: 68.7 us -> none  [the longest x1 60 us: body(): lax.all_to_all(outgoing, 'enc', split_axis=0, concat_axis=0, tiled=True)]
    all_to_all x2 -> x0, starting transfers between devices: 16.8 us -> none  [the longest x1 12.1 us: body(): lax.all_to_all(outgoing, 'enc', split_axis=0, concat_axis=0, tiled=True)]
    reduce_sum x7 -> x1, other arithmetic: 16 us -> 0.48 us  [body(): present = jnp.sum(taken, axis=2).reshape(-1)]
    dot_general x9 -> x0, matrix products: 13.9 us -> none  [the longest x1 3.45 us: body(): jnp.einsum('skrp,skrd->pd', received, d_proj_low, preferred_element_type=...]
  transfers between devices with their start and end apart: 3 -> 0, of which waited for: 3 -> 0; matrix products, arithmetic and copies ran while one was open for 1% -> 0% of each run, Pallas kernels for 0% -> 0%
where the time goes in v2:
time: 109 us
  Pallas kernels  97.7 us (90%)
  local copies, waits for them, and re-layouts  6.79 us (6%)
  other arithmetic  3.01 us (3%)
  between operations  1.42 us (1%)
    pallas_call x1, Pallas kernels, train_step(): pl.pallas_call(step_kernel, out_shape=(jax.ShapeDtypeStruct((USERS_DEV, D...  97.7 us
    unnamed x19, local copies, waits for them, and re-layouts  6.45 us

profile of v2, /device:TPU:6, one launch (start us, length us, event | category | flops | bytes accessed | tf_op | source)
XLA Modules:
  0.0 108.9 jit_solution(15652446488825793494)
XLA Ops:
  1.3 0.8 and_select_fusion
  2.2 0.9 fusion.3
  3.1 0.7 fusion.1
  3.8 0.5 convert_reduce_fusion
  4.3 0.1 gt.11
  4.4 0.1 reshape.310.src_ref
  4.5 0.1 broadcast_in_dim.7
  4.6 0.1 reshape.311.items_ref
  4.7 0.0 copy-start
  4.7 0.0 copy-start.1
  4.7 0.0 copy-start.4
  4.7 0.0 copy-start.5
  4.7 0.0 copy-start.6
  4.8 1.6 %copy.19.patches_ref = bf16[4,196,768]{2,1,0:T(8,128)(2,1)S(1)} copy(bf16[4,196,768]{2,0,1:T(4,128)(2,1)} %param.11) | data formatting | bytes 2408448 | tf_op args[0]
  6.3 0.0 copy-done
  6.3 0.4 copy-done.1
  6.7 0.0 copy-done.4
  6.7 0.0 copy-done.5
  6.7 0.0 copy-done.6
  6.7 0.0 copy-start.2
  6.7 1.0 copy-done.2
  7.7 0.0 copy-start.3
  7.7 0.9 copy-done.3
  8.7 97.7 %train_step.1 = (bf16[256,768]{1,0:T(8,128)(2,1)S(1)}, f32[12,768]{1,0:T(8,128)S(1)}, f32[1,768]{1,0:T(1,128)S(1)}, f32[1,768]{1,0:T(1,128)S(1)}) custom-call(s32[24]{0:T(128)S(1)} %reshape.310.src_ref, s32[4]{0:T(128)S(1)} %copy-done.6, s32[1]{0:T(128)} %copy.24.live_ref, s32[1,192]{1,0:T(1,128)S(1)} %reshape.311.items_ref, s32[1,256]{1,0:T(1,128)S(1)} %bitcast.11, ...), custom_call_target="tpu_custom_call" | custom-call | tf_op jit(solution)/shard_map/train_step/pallas_call | solution.py:403
  106.3 0.7 copy.20
  107.0 0.7 copy.25
  107.8 0.6 copy.26
  108.3 0.6 copy.27
  (5 shorter events, 0.1 us)
Async XLA Ops:
  4.7 1.6 %copy-start = (bf16[1,768,768]{2,1,0:T(8,128)(2,1)S(1)}, bf16[1,768,768]{2,1,0:T(8,128)(2,1)}, u32[]{:S(2)}) copy-start(bf16[1,768,768]{2,1,0:T(8,128)(2,1)} %param.15) | copy-start | bytes 3538948
  4.7 2.0 %copy-start.1 = (bf16[768,768]{1,0:T(8,128)(2,1)S(1)}, bf16[768,768]{1,0:T(8,128)(2,1)}, u32[]{:S(2)}) copy-start(bf16[768,768]{1,0:T(8,128)(2,1)} %proj_ref.1) | copy-start | bytes 3538948
  4.7 2.0 %copy-start.4 = (f32[1,768]{1,0:T(1,128)S(1)}, f32[1,768]{1,0:T(1,128)}, u32[]{:S(2)}) copy-start(f32[1,768]{1,0:T(1,128)} %bias_ref.1) | copy-start | bytes 9220
  4.7 2.0 %copy-start.5 = (f32[1,768]{1,0:T(1,128)S(1)}, f32[1,768]{1,0:T(1,128)}, u32[]{:S(2)}) copy-start(f32[1,768]{1,0:T(1,128)} %gain_ref.1) | copy-start | bytes 9220
  4.7 2.0 %copy-start.6 = (s32[4]{0:T(128)S(1)}, s32[4]{0:T(128)}, u32[]{:S(2)}) copy-start(s32[4]{0:T(128)} %ids_ref.1) | copy-start | bytes 52
  6.7 1.0 copy-start.2
  7.7 0.9 copy-start.3

commit v3 on v2

--- a/solution.py
+++ b/solution.py
@@ -18,7 +18,9 @@
 MAIN = 48
 NX, NY, NZ = 4, 8, 2
 ROWS_DEV = 12
-FOLD = 1152
+PIECE = 256
+N_PIECES = D // PIECE
+FOLD = 384
 LANES = 128
 PIECES = D // LANES
 GROUP = 16
@@ -35,12 +37,12 @@
 
 def fold(rows):
     tail = rows[8:12]
-    return jnp.concatenate([rows[0:8], jnp.concatenate([tail[:, :384], tail[:, 384:]], axis=0)], axis=1)
+    return jnp.concatenate([rows[0:8], jnp.concatenate([tail[:, :LANES], tail[:, LANES:]], axis=0)], axis=1)
 
 
 def unfold(folded):
-    tail = folded[:, 768:]
-    return jnp.concatenate([folded[:, :768], jnp.concatenate([tail[0:4], tail[4:8]], axis=1)], axis=0)
+    tail = folded[:, PIECE:]
+    return jnp.concatenate([folded[:, :PIECE], jnp.concatenate([tail[0:4], tail[4:8]], axis=1)], axis=0)
 
 
 def row_to_tile(row):
@@ -84,14 +86,15 @@
 
 
 def step_kernel(
-    src_ref, ids_ref, live_ref, items_ref, chosen_ref, patches_ref, w_ref, bias_ref, gain_ref, ibias_ref,
-    users_ref, proj_ref,
+    blocks_ref, ids_ref, live_ref, positives_ref, patches_ref, w_hbm, bias_ref, gain_ref, ibias_hbm,
+    users_hbm, proj_hbm,
     duser_ref, out_ref, bout_ref, gout_ref,
     main, tails, send, recv, tsend, trecv, trows, xtail, psend, precv, dsend, drecv,
     proj, xhat_m, slope_m, rstd_m, act_t, xhat_t, slope_t, rstd_t, dtail, gsum, dlow, dlow_t, uvec, dbacc, g,
-    sx, rx, sy, ry, accx, sz, rz, vown, vx, vy, vz,
+    w_ref, ibias_ref, users_ref, proj_ref, proj_t, xt, xt_t,
+    sx, rx, relay, sy, ry, accx, sz, rz, vown, vx, vy, vz,
     sem_s, sem_r, sem_ts, sem_tr, sem_ps, sem_pr, sem_ds, sem_dr,
-    sem_sx, sem_rx, sem_sy, sem_ry, sem_z, sem_vsx, sem_vrx, sem_vsy, sem_vry, sem_vz,
+    sem_sx, sem_rx, sem_sy, sem_ry, sem_z, sem_vsx, sem_vrx, sem_vsy, sem_vry, sem_vz, sem_load,
 ):
     dp = lax.axis_index("dp")
     enc = lax.axis_index("enc")
@@ -115,6 +118,11 @@
         other = (core + r) % 2
         return on_ring(ring - offset(p, other), other)
 
+    loads = [
+        pltpu.make_async_copy(there, here, sem_load.at[n])
+        for n, (there, here) in enumerate(
+            [(users_hbm, users_ref), (proj_hbm, proj_ref), (ibias_hbm, ibias_ref), (w_hbm, w_ref)])
+    ]
     barrier = pltpu.get_barrier_semaphore()
     partners = 0
     for p in range(6):
@@ -128,6 +136,25 @@
         pl.semaphore_signal(barrier, inc=1, device_id=at(x, (y + d) % NY, z))
     pl.semaphore_signal(barrier, inc=1, device_id=at(x, y, 1 - z))
     partners += NX + NY - 1
+    for load in loads:
+        load.start()
+
+    n_live = live_ref[0] * BLOCKS_ITEM
+    named = [jnp.where(b < n_live, blocks_ref[b], -1) for b in range(BLOCKS_DEV)]
+    src = []
+    lane_slot = lax.broadcasted_iota(jnp.int32, (1, N_ENC * 16), 1) >> 3
+    items = jnp.full((1, N_ENC * 16), -1, jnp.int32)
+    for j in range(N_ENC):
+        expert = dest(j // 2, j % 2)["enc"]
+        low, high = jnp.int32(BLOCKS_DEV), jnp.int32(-1)
+        for b in range(BLOCKS_DEV):
+            high = jnp.where(named[b] == expert, b, high)
+            back = BLOCKS_DEV - 1 - b
+            low = jnp.where(named[back] == expert, back, low)
+        src.append(jnp.minimum(low, BLOCKS_DEV - 1))
+        src.append(jnp.maximum(high, 0))
+        items = jnp.where(lane_slot == 2 * j, jnp.where(low < BLOCKS_DEV, low >> 2, -1), items)
+        items = jnp.where(lane_slot == 2 * j + 1, jnp.where(high > low, high >> 2, -1), items)
 
     tails[...] = jnp.zeros_like(tails)
     row = lax.broadcasted_iota(jnp.int32, (208, PATCHES), 0)
@@ -136,7 +163,7 @@
     origin = jnp.where(row < 192, row + steps, (row - 192) * BLOCK_ROWS + MAIN)
     order = jnp.where(origin == col, 1.0, 0.0).astype(bf16)
     for i in range(ITEMS_DEV):
-        sorted_rows = jnp.dot(order, patches_ref[i], preferred_element_type=f32)
+        sorted_rows = jnp.dot(order, patches_ref[:, i, :], preferred_element_type=f32)
         for b in range(BLOCKS_ITEM):
             main[i * BLOCKS_ITEM + b] = sorted_rows[b * MAIN : (b + 1) * MAIN].astype(bf16)
             tails[i * BLOCKS_ITEM + b] = row_to_tile(sorted_rows[192 + b : 193 + b])
@@ -146,7 +173,7 @@
             src_ref=src, dst_ref=dst, send_sem=ssem, recv_sem=rsem, device_id=device)
 
     def tail_tile(j):
-        return jnp.concatenate([tails[src_ref[2 * j]], tails[src_ref[2 * j + 1]]], axis=0).astype(bf16)
+        return jnp.concatenate([tails[src[2 * j]], tails[src[2 * j + 1]]], axis=0).astype(bf16)
 
     trecv[0] = tail_tile(0)
     for j in range(1, N_ENC):
@@ -166,16 +193,24 @@
             j = 2 * p + r
             if j:
                 for k in range(CAP):
-                    send[j, k] = main[src_ref[2 * j + k]]
+                    send[j, k] = main[src[2 * j + k]]
                 start(remote(send.at[j], recv.at[j], sem_s.at[j], sem_r.at[j], dest(p, r)))
     for k in range(CAP):
-        recv[0, k] = main[src_ref[k]]
+        recv[0, k] = main[src[k]]
+
+    for load in loads:
+        load.wait()
 
     @pl.loop(0, D // 256)
     def _(m):
         first = pl.multiple_of(m * 256, 256)
         uvec[:, pl.ds(first, 256)] = jnp.dot(
             users_ref[...], proj_ref[:, pl.ds(first, 256)], preferred_element_type=f32).astype(bf16)
+
+    @pl.loop(0, PIECES)
+    def _(c):
+        lanes = pl.ds(pl.multiple_of(c * LANES, LANES), LANES)
+        proj_t[lanes, :] = proj_ref[:, lanes].T
 
     entry = lax.broadcasted_iota(jnp.int32, (512, LANES), 0) * LANES + lax.broadcasted_iota(jnp.int32, (512, LANES), 1)
     item_row = lax.broadcasted_iota(jnp.int32, (8, 1), 0)
@@ -187,7 +222,7 @@
 
     out_row = lax.broadcasted_iota(jnp.int32, (48, N_ENC * 16), 0)
     in_col = lax.broadcasted_iota(jnp.int32, (48, N_ENC * 16), 1)
-    belongs = ((out_row & 7) == items_ref[...]) & ((out_row >> 3) == (in_col & 7))
+    belongs = ((out_row & 7) == items) & ((out_row >> 3) == (in_col & 7))
     belongs = jnp.where(belongs, 1.0, 0.0).astype(bf16)
 
     bias = bias_ref[...]
@@ -201,6 +236,7 @@
         for k in range(CAP):
             trows[2 * j + k : 2 * j + k + 1, :] = tile_to_row(tile[8 * k : 8 * k + 8])
     xtail[...] = trows[...].astype(bf16)
+    xt_t[...] = trows[...].T.astype(bf16)
     proj[0:32, :] = jnp.dot(xtail[...], w_ref[...], preferred_element_type=f32)
     for s in range(2):
         rows = slice(s * GROUP, (s + 1) * GROUP)
@@ -261,6 +297,12 @@
     lax.fori_loop(0, 6, forward, 0)
 
     returned = [remote(psend.at[j], precv.at[j], sem_ps.at[j], sem_pr.at[j], source(j // 2, j % 2)) for j in range(1, N_ENC)]
+
+    def turn(c, carry):
+        lanes = pl.ds(pl.multiple_of(c * LANES, LANES), LANES)
+        xt[lanes, :] = recv[:, :, :, lanes].reshape(SLOTS * MAIN, LANES).T
+        return carry
+    lax.fori_loop(0, PIECES // 2, turn, 0)
     for copy in returned:
         copy.wait_recv()
     summed = jnp.dot(belongs, precv[...].reshape(N_ENC * 16, LANES), preferred_element_type=f32)
@@ -269,7 +311,11 @@
     scores = lax.dot_general(embed, uvec[...], (((1,), (1,)), ((), ())), preferred_element_type=f32)
     scores = scores * score_scale + item_biases
     index = lax.broadcasted_iota(jnp.int32, (8, USERS_DEV), 0)
-    target = jnp.where(index == chosen_ref[...], 1.0, 0.0)
+    chosen = positives_ref[...].astype(f32)
+    chosen = jnp.concatenate([chosen[0:1], chosen[1:2]], axis=1)
+    live = live_ref[0].astype(f32)
+    chosen = chosen - live * jnp.floor((chosen + 0.5) / live)
+    target = jnp.where(index.astype(f32) == chosen, 1.0, 0.0)
     sigmoid = 1.0 / (1.0 + jnp.exp(-scores))
     d_score = jnp.where(index < live_ref[0], loss_weight * (sigmoid - target), 0.0).astype(bf16)
     d_embed = jnp.dot(d_score, uvec[...], preferred_element_type=f32) * score_scale
@@ -282,14 +328,7 @@
             if j:
                 start(remote(dsend.at[j], drecv.at[j], sem_ds.at[j], sem_dr.at[j], dest(p, r)))
     drecv[0] = dsend[0]
-    d_user_vec = lax.dot_general(d_score, embed, (((0,), (0,)), ((), ())), preferred_element_type=f32)
-    uvec[...] = (d_user_vec * score_scale).astype(bf16)
-
-    @pl.loop(0, D // 256)
-    def _(m):
-        first = pl.multiple_of(m * 256, 256)
-        duser_ref[:, pl.ds(first, 256)] = lax.dot_general(
-            uvec[...], proj_ref[pl.ds(first, 256), :], (((1,), (1,)), ((), ())), preferred_element_type=f32).astype(bf16)
+    lax.fori_loop(PIECES // 2, PIECES, turn, 0)
 
     dtail[...] = jnp.zeros_like(dtail)
     dbacc[...] = jnp.zeros_like(dbacc)
@@ -323,92 +362,168 @@
     d_gain = jnp.sum(dtail[0:SLOTS, :] * gsum[0:SLOTS, :], axis=0, keepdims=True)
     vectors = jnp.concatenate([row_to_tile(d_bias), row_to_tile(d_gain)], axis=0)
 
-    @pl.loop(0, D // 256)
-    def _(m):
-        first = pl.multiple_of(m * 256, 256)
-        g[pl.ds(first, 256), :] = lax.dot_general(
-            recv[:, :, :, pl.ds(first, 256)].reshape(SLOTS * MAIN, 256), dlow[...].reshape(SLOTS * MAIN, D),
-            (((0,), (0,)), ((), ())), preferred_element_type=f32) + lax.dot_general(
-            xtail[:, pl.ds(first, 256)], dlow_t[...], (((0,), (0,)), ((), ())), preferred_element_type=f32)
-
-    for copy in started + returned:
-        copy.wait_send()
-
     vown[...] = vectors
-
-    def pack(xx):
+    vx[x] = vectors
+    vectors_x = [remote(vown, vx.at[x], sem_vsx.at[d - 1], sem_vrx.at[d - 1], at((x + d) % NX, y, z)) for d in range(1, NX)]
+    for copy in vectors_x:
+        copy.start()
+
+    def pack(h, xx):
         @pl.loop(0, NY)
         def _(k):
             first = pl.multiple_of((xx * NY + k) * 24, 8)
             chunk = g[pl.ds(first, 24), :]
-            sx[xx, k] = jnp.concatenate([fold(chunk[0:12]), fold(chunk[12:24])], axis=0).astype(bf16)
-
-    vx[x] = vectors
-    firsts = []
-    for d in range(1, NX):
-        to = (x + d) % NX
-        pack(to)
-        firsts.append(remote(sx.at[to], rx.at[d - 1], sem_sx.at[d - 1], sem_rx.at[d - 1], at(to, y, z)))
-        firsts.append(remote(vown, vx.at[x], sem_vsx.at[d - 1], sem_vrx.at[d - 1], at(to, y, z)))
-        firsts[-2].start()
-        firsts[-1].start()
-    pack(x)
-    for copy in firsts:
+            sx[h, xx, k] = jnp.concatenate([fold(chunk[0:12]), fold(chunk[12:24])], axis=0).astype(bf16)
+
+    left, right, far = (x + 3) % NX, (x + 1) % NX, (x + 2) % NX
+    low, high = pl.ds(0, NY // 2), pl.ds(NY // 2, NY // 2)
+
+    def along_x(h, n):
+        source_ref, to = [
+            (sx.at[h, far, low], left), (sx.at[h, far, high], right),
+            (sx.at[h, right, low], right), (sx.at[h, left, high], left),
+            (relay.at[h, 0], left), (relay.at[h, 1], right),
+        ][n]
+        return remote(source_ref, rx.at[h, n], sem_sx.at[h, n], sem_rx.at[h, n], at(to, y, z))
+
+    def pass_on(h):
+        for n in range(2):
+            along_x(h, n).wait_recv()
+            half = sx[h, left, low] if n == 0 else sx[h, right, high]
+            relay[h, n] = (rx[h, n].astype(f32) + half.astype(f32)).astype(bf16)
+            along_x(h, 4 + n).start()
+
+    def along_y(h, d):
+        to = (y + d) % NY
+        return remote(sy.at[h, to], ry.at[h, d - 1], sem_sy.at[h, d - 1], sem_ry.at[h, d - 1], at(x, to, z))
+
+    def along_z(h):
+        return remote(sz.at[h, 1 - z], rz.at[h], sem_z.at[h, 0], sem_z.at[h, 1], at(x, y, 1 - z))
+
+    vectors_y = [remote(vy.at[y], vy.at[y], sem_vsy.at[d - 1], sem_vry.at[d - 1], at(x, (y + d) % NY, z)) for d in range(1, NY)]
+    vectors_z = remote(vz.at[0], vz.at[1], sem_vz.at[0], sem_vz.at[1], at(x, y, 1 - z))
+
+    def piece(h, carry):
+        lanes = pl.ds(pl.multiple_of(h * PIECE, PIECE), PIECE)
+        g[...] = jnp.dot(
+            xt[...], dlow[:, :, lanes].reshape(SLOTS * MAIN, PIECE), preferred_element_type=f32) + jnp.dot(
+            xt_t[...], dlow_t[:, lanes], preferred_element_type=f32)
+        pack(h, far)
+        along_x(h, 0).start()
+        along_x(h, 1).start()
+        pack(h, right)
+        along_x(h, 2).start()
+        pack(h, left)
+        along_x(h, 3).start()
+        pack(h, x)
+
+        @pl.when(h > 0)
+        def _():
+            pass_on(h - 1)
+        return carry
+    lax.fori_loop(0, N_PIECES, piece, 0)
+
+    def sum_x(h):
+        for n in range(2, 6):
+            along_x(h, n).wait_recv()
+
+        @pl.loop(0, NY // 2)
+        def _(k):
+            for n in range(2):
+                own = k + n * (NY // 2)
+                total = sx[h, x, own].astype(f32) + (rx[h, 2 + n, k].astype(f32) + rx[h, 4 + n, k].astype(f32))
+                accx[h, own] = total
+                sy[h, own] = total.astype(bf16)
+        for d in range(1, NY):
+            along_y(h, d).start()
+
+    def sum_y(h):
+        total = accx[h, y]
+        for d in range(1, NY):
+            along_y(h, d).wait_recv()
+            total = total + ry[h, d - 1].astype(f32)
+        sz[h, 0] = total[0:8]
+        sz[h, 1] = total[8:16]
+        along_z(h).start()
+
+    for copy in vectors_x:
         copy.wait_recv()
     vy[y] = (vx[0] + vx[1]) + (vx[2] + vx[3])
-
-    def sum_x(k, carry):
-        total = (sx[x, k].astype(f32) + rx[0, k].astype(f32)) + (rx[1, k].astype(f32) + rx[2, k].astype(f32))
-        accx[k] = total
-        sy[k] = total.astype(bf16)
-        return carry
-    lax.fori_loop(0, NY, sum_x, 0)
-    second = []
-    for d in range(1, NY):
-        to = (y + d) % NY
-        second.append(remote(sy.at[to], ry.at[d - 1], sem_sy.at[d - 1], sem_ry.at[d - 1], at(x, to, z)))
-        second.append(remote(vy.at[y], vy.at[y], sem_vsy.at[d - 1], sem_vry.at[d - 1], at(x, to, z)))
-        second[-2].start()
-        second[-1].start()
-    total = accx[y]
-    for d in range(1, NY):
-        second[2 * d - 2].wait_recv()
-        total = total + ry[d - 1].astype(f32)
-    for d in range(1, NY):
-        second[2 * d - 1].wait_recv()
+    for copy in vectors_y:
+        copy.start()
+    pass_on(N_PIECES - 1)
+    sum_x(0)
+    sum_x(1)
+    d_user_vec = lax.dot_general(d_score, embed, (((0,), (0,)), ((), ())), preferred_element_type=f32)
+    uvec[...] = (d_user_vec * score_scale).astype(bf16)
+
+    @pl.loop(0, D // 256)
+    def _(m):
+        lanes = pl.ds(pl.multiple_of(m * 256, 256), 256)
+        duser_ref[:, lanes] = jnp.dot(uvec[...], proj_t[:, lanes], preferred_element_type=f32).astype(bf16)
+
+    sum_x(2)
+    for copy in vectors_y:
+        copy.wait_recv()
     vz[0] = ((vy[0] + vy[1]) + (vy[2] + vy[3])) + ((vy[4] + vy[5]) + (vy[6] + vy[7]))
-    sz[0] = total[0:8]
-    sz[1] = total[8:16]
-    last = [
-        remote(sz.at[1 - z], rz, sem_z.at[0], sem_z.at[1], at(x, y, 1 - z)),
-        remote(vz.at[0], vz.at[1], sem_vz.at[0], sem_vz.at[1], at(x, y, 1 - z)),
-    ]
-    for copy in last:
-        copy.start()
-    for copy in last:
-        copy.wait_recv()
+    vectors_z.start()
+    for h in range(N_PIECES):
+        sum_y(h)
     scale = 1.0 / (NX * NY * NZ)
-    out_ref[...] = unfold((sz[z] + rz[...]) * scale)
+    vectors_z.wait_recv()
     folded = (vz[0] + vz[1]) * scale
     bout_ref[...] = tile_to_row(folded[0:8])
     gout_ref[...] = tile_to_row(folded[8:16])
-    for copy in firsts + second + last:
+    for h in range(N_PIECES):
+        along_z(h).wait_recv()
+        rows = unfold((sz[h, z] + rz[h]) * scale)
+        for r in range(ROWS_DEV):
+            out_ref[r, :, h * PIECE : (h + 1) * PIECE] = rows[r : r + 1]
+    for copy in started + returned + vectors_x + vectors_y + [vectors_z]:
         copy.wait_send()
-
-
-def train_step(src, ids, live, items, chosen, patches, weight, bias, gain, item_bias, users, proj):
+    for h in range(N_PIECES):
+        for n in range(6):
+            along_x(h, n).wait_send()
+        for d in range(1, NY):
+            along_y(h, d).wait_send()
+        along_z(h).wait_send()
+
+
+def copy_kernel(*refs):
+    n = len(refs) // 2
+    copies = [pltpu.make_async_copy(refs[i], refs[n + i], refs[-1].at[i]) for i in range(n)]
+    for copy in copies:
+        copy.start()
+    for copy in copies:
+        copy.wait()
+
+
+def copy_out(arrays):
+    return pl.pallas_call(
+        copy_kernel,
+        out_shape=[jax.ShapeDtypeStruct(a.shape, a.dtype) for a in arrays],
+        in_specs=[pl.BlockSpec(memory_space=pltpu.VMEM)] * len(arrays),
+        out_specs=[pl.BlockSpec(memory_space=pl.ANY)] * len(arrays),
+        scratch_shapes=[pltpu.SemaphoreType.DMA((len(arrays),))],
+        compiler_params=pltpu.CompilerParams(vmem_limit_bytes=60 * 1024 * 1024),
+        name="copy_out",
+    )(*arrays)
+
+
+def train_step(blocks, ids, live, positives, patches, weight, bias, gain, item_bias, users, proj):
     vmem = pl.BlockSpec(memory_space=pltpu.VMEM)
     smem = pl.BlockSpec(memory_space=pltpu.SMEM)
+    anywhere = pl.BlockSpec(memory_space=pl.ANY)
     dma = pltpu.SemaphoreType.DMA
     return pl.pallas_call(
         step_kernel,
         out_shape=(
             jax.ShapeDtypeStruct((USERS_DEV, D), bf16),
-            jax.ShapeDtypeStruct((ROWS_DEV, D), f32),
+            jax.ShapeDtypeStruct((ROWS_DEV, 1, D), f32),
             jax.ShapeDtypeStruct((1, D), f32),
             jax.ShapeDtypeStruct((1, D), f32),
         ),
-        in_specs=[smem] * 3 + [vmem] * 9,
+        in_specs=[smem] * 3 + [vmem] * 2 + [anywhere] + [vmem] * 2 + [anywhere] * 3,
         out_specs=[vmem] * 4,
         scratch_shapes=[
             pltpu.VMEM((BLOCKS_DEV, MAIN, D), bf16),
@@ -433,26 +548,35 @@
             pltpu.VMEM((32, D), bf16),
             pltpu.VMEM((USERS_DEV, D), bf16),
             pltpu.VMEM((8, D), f32),
-            pltpu.VMEM((D, D), f32),
-            pltpu.VMEM((NX, NY, 16, FOLD), bf16),
-            pltpu.VMEM((NX - 1, NY, 16, FOLD), bf16),
-            pltpu.VMEM((NY, 16, FOLD), bf16),
-            pltpu.VMEM((NY - 1, 16, FOLD), bf16),
-            pltpu.VMEM((NY, 16, FOLD), f32),
-            pltpu.VMEM((2, 8, FOLD), f32),
-            pltpu.VMEM((8, FOLD), f32),
+            pltpu.VMEM((D, PIECE), f32),
+            pltpu.VMEM((D, D), bf16),
+            pltpu.VMEM((512, LANES), f32),
+            pltpu.VMEM((USERS_DEV, D), bf16),
+            pltpu.VMEM((D, D), bf16),
+            pltpu.VMEM((D, D), bf16),
+            pltpu.VMEM((D, SLOTS * MAIN), bf16),
+            pltpu.VMEM((D, 32), bf16),
+            pltpu.VMEM((N_PIECES, NX, NY, 16, FOLD), bf16),
+            pltpu.VMEM((N_PIECES, 6, NY // 2, 16, FOLD), bf16),
+            pltpu.VMEM((N_PIECES, 2, NY // 2, 16, FOLD), bf16),
+            pltpu.VMEM((N_PIECES, NY, 16, FOLD), bf16),
+            pltpu.VMEM((N_PIECES, NY - 1, 16, FOLD), bf16),
+            pltpu.VMEM((N_PIECES, NY, 16, FOLD), f32),
+            pltpu.VMEM((N_PIECES, 2, 8, FOLD), f32),
+            pltpu.VMEM((N_PIECES, 8, FOLD), f32),
             pltpu.VMEM((16, LANES), f32),
             pltpu.VMEM((NX, 16, LANES), f32),
             pltpu.VMEM((NY, 16, LANES), f32),
             pltpu.VMEM((2, 16, LANES), f32),
         ] + [dma((N_ENC,))] * 8 + [
-            dma((NX - 1,)), dma((NX - 1,)), dma((NY - 1,)), dma((NY - 1,)), dma((2,)),
-            dma((NX - 1,)), dma((NX - 1,)), dma((NY - 1,)), dma((NY - 1,)), dma((2,)),
+            dma((N_PIECES, 6)), dma((N_PIECES, 6)), dma((N_PIECES, NY - 1)), dma((N_PIECES, NY - 1)),
+            dma((N_PIECES, 2)),
+            dma((NX - 1,)), dma((NX - 1,)), dma((NY - 1,)), dma((NY - 1,)), dma((2,)), dma((4,)),
         ],
         compiler_params=pltpu.CompilerParams(
-            collective_id=0, has_side_effects=True, vmem_limit_bytes=48 * 1024 * 1024),
+            collective_id=0, has_side_effects=True, vmem_limit_bytes=56 * 1024 * 1024),
         name="train_step",
-    )(src, ids, live, items, chosen, patches, weight, bias, gain, item_bias, users, proj)
+    )(blocks, ids, live, positives, patches, weight, bias, gain, item_bias, users, proj)
 
 
 def body(
@@ -468,27 +592,11 @@
     user_proj,
     positives,
 ):
-    enc = lax.axis_index("enc")
-    core = enc % 2
-    live_items = item_counts[0]
-    place = jnp.arange(N_ENC, dtype=jnp.int32)
-    chip = (enc // 2 + offset(place // 2, core) + 6) % 6
-    expert = chip * 2 + (core + place % 2) % 2
-    number = jnp.arange(BLOCKS_DEV, dtype=jnp.int32)
-    live_block = number // BLOCKS_ITEM < live_items
-    routed = (block_dest[None, :] == expert[:, None]) & live_block[None, :]
-    earlier = (block_dest[None, :] == block_dest[:, None]) & (number[None, :] < number[:, None])
-    second = jnp.any(earlier, axis=1)
-    taken = jnp.stack([routed & ~second[None, :], routed & second[None, :]], axis=1).astype(jnp.int32)
-    src = jnp.sum(taken * number[None, None, :], axis=2).reshape(-1)
-    present = jnp.sum(taken, axis=2).reshape(-1)
-    item = jnp.where(present > 0, src // BLOCKS_ITEM, -1)
-    items = jnp.broadcast_to(item[:, None], (SLOTS, 8)).reshape(1, SLOTS * 8)
-    chosen = (positives % live_items)[None, :]
-    d_user, mine, d_bias, d_gain = train_step(
-        src, item_ids, item_counts, items, chosen, patches, enc_weight[0], enc_bias, enc_gain,
+    outs = train_step(
+        block_dest, item_ids, item_counts, positives.reshape(-1, LANES), jnp.transpose(patches, (1, 0, 2)), enc_weight[0], enc_bias, enc_gain,
         item_bias.reshape(-1, LANES), user_state, user_proj)
-    return (d_user, mine[None], d_bias, d_gain)
+    d_user, mine, d_bias, d_gain = copy_out(outs)
+    return (d_user, jnp.transpose(mine, (1, 0, 2)), d_bias, d_gain)
 
 
 def solution(mesh):

time: 109 us -> 95.1 us (0.87)
  local copies, waits for them, and re-layouts: 6.79 us -> 0 us
  Pallas kernels: 97.7 us -> 92.9 us
  other arithmetic: 3.01 us -> 0 us
    pallas_call x1, Pallas kernels: 97.7 us -> 91.1 us  [train_step(): pl.pallas_call(step_kernel, out_shape=(jax.ShapeDtypeStruct((USERS_DEV, D...]
    unnamed x19 -> x0, local copies, waits for them, and re-layouts: 6.45 us -> none
    pallas_call x0 -> x1, Pallas kernels: none -> 1.81 us  [copy_out(): pl.pallas_call(copy_kernel, out_shape=[jax.ShapeDtypeStruct(a.shape, a.dt...]
where the time goes in v3:
time: 95.1 us; the launch traced here: 94.2 us
  Pallas kernels  92.9 us (98%)
  between operations  1.29 us (1%)
    pallas_call x1, Pallas kernels, train_step(): pl.pallas_call(step_kernel, out_shape=(jax.ShapeDtypeStruct((USERS_DEV, D...  91.1 us

profile of v3, /device:TPU:6, one launch (start us, length us, event | category | flops | bytes accessed | tf_op | source)
XLA Modules:
  0.0 94.2 jit_solution(5383574363603543013)
XLA Ops:
  1.3 91.1 %train_step.1 = (bf16[256,768]{1,0:T(8,128)(2,1)}, f32[12,1,768]{2,1,0:T(1,128)}, f32[1,768]{1,0:T(1,128)}, f32[1,768]{1,0:T(1,128)}) custom-call(s32[16]{0:T(128)} %blocks_ref.1, s32[4]{0:T(128)} %ids_ref.1, s32[1]{0:T(128)S(6)} %copy.15.live_ref, s32[2,128]{1,0:T(2,128)} %bitcast.8, bf16[196,4,768]{2,1,0:T(4,128)(2,1)} %bitcast.5, ...), custom_call_target="tpu_custom_call" | custom-call | tf_op jit(solution)/shard_map/train_step/pallas_call | solution.py:518
  92.4 1.8 %copy_out.1 = (bf16[256,768]{1,0:T(8,128)(2,1)}, f32[12,1,768]{2,1,0:T(1,128)}, f32[1,768]{1,0:T(1,128)}, f32[1,768]{1,0:T(1,128)}) custom-call(bf16[256,768]{1,0:T(8,128)(2,1)} %get-tuple-element.12.refs_0_, f32[12,1,768]{2,1,0:T(1,128)} %get-tuple-element.13.refs_1_, f32[1,768]{1,0:T(1,128)} %get-tuple-element.14.refs_2_, f32[1,768]{1,0:T(1,128)} %get-tuple-element.15.refs_3_), custom_call_target="tpu_custom_call" | custom-call | tf_op jit(solution)/shard_map/copy_out/pallas_call | solution.py:502

commit v4 on v3

--- a/solution.py
+++ b/solution.py
@@ -91,7 +91,7 @@
     duser_ref, out_ref, bout_ref, gout_ref,
     main, tails, send, recv, tsend, trecv, trows, xtail, psend, precv, dsend, drecv,
     proj, xhat_m, slope_m, rstd_m, act_t, xhat_t, slope_t, rstd_t, dtail, gsum, dlow, dlow_t, uvec, dbacc, g,
-    w_ref, ibias_ref, users_ref, proj_ref, proj_t, xt, xt_t,
+    w_ref, ibias_ref, users_ref, proj_ref, proj_t, uvec_t, belongs_t, xt, xt_t,
     sx, rx, relay, sy, ry, accx, sz, rz, vown, vx, vy, vz,
     sem_s, sem_r, sem_ts, sem_tr, sem_ps, sem_pr, sem_ds, sem_dr,
     sem_sx, sem_rx, sem_sy, sem_ry, sem_z, sem_vsx, sem_vrx, sem_vsy, sem_vry, sem_vz, sem_load,
@@ -186,9 +186,10 @@
         started.append(copy)
         return copy
 
-    for j in range(1, N_ENC):
-        start(remote(tsend.at[j], trecv.at[j], sem_ts.at[j], sem_tr.at[j], dest(j // 2, j % 2)))
     for p in (5, 4, 3, 2, 1, 0):
+        if p == 5:
+            for j in range(1, N_ENC):
+                start(remote(tsend.at[j], trecv.at[j], sem_ts.at[j], sem_tr.at[j], dest(j // 2, j % 2)))
         for r in range(2):
             j = 2 * p + r
             if j:
@@ -224,6 +225,10 @@
     in_col = lax.broadcasted_iota(jnp.int32, (48, N_ENC * 16), 1)
     belongs = ((out_row & 7) == items) & ((out_row >> 3) == (in_col & 7))
     belongs = jnp.where(belongs, 1.0, 0.0).astype(bf16)
+
+    belongs_t[...] = belongs.astype(f32).T.astype(bf16)
+    for c in range(PIECES):
+        uvec_t[c * LANES : (c + 1) * LANES, :] = uvec[:, c * LANES : (c + 1) * LANES].T
 
     bias = bias_ref[...]
     gain = gain_ref[...]
@@ -279,7 +284,7 @@
             gsum[pl.ds(own, 1), :] = jnp.sum(gs, axis=0, keepdims=True) + weighted
             trows[pl.ds(own, 1), :] = jnp.sum(pool, axis=0, keepdims=True) + pooled
             return carry
-        lax.fori_loop(0, 4, slot, 0)
+        lax.fori_loop(0, 4, slot, 0, unroll=True)
         for r in range(2):
             j = 2 * p + r
             tile = jnp.concatenate(
@@ -308,7 +313,7 @@
     summed = jnp.dot(belongs, precv[...].reshape(N_ENC * 16, LANES), preferred_element_type=f32)
     embed = jnp.concatenate([summed[8 * c : 8 * c + 8] for c in range(PIECES)], axis=1)
     embed = (embed / PATCHES).astype(bf16)
-    scores = lax.dot_general(embed, uvec[...], (((1,), (1,)), ((), ())), preferred_element_type=f32)
+    scores = jnp.dot(embed, uvec_t[...], preferred_element_type=f32)
     scores = scores * score_scale + item_biases
     index = lax.broadcasted_iota(jnp.int32, (8, USERS_DEV), 0)
     chosen = positives_ref[...].astype(f32)
@@ -320,7 +325,7 @@
     d_score = jnp.where(index < live_ref[0], loss_weight * (sigmoid - target), 0.0).astype(bf16)
     d_embed = jnp.dot(d_score, uvec[...], preferred_element_type=f32) * score_scale
     d_folded = jnp.concatenate([d_embed[:, c * LANES : (c + 1) * LANES] for c in range(PIECES)], axis=0).astype(bf16)
-    d_slots = lax.dot_general(belongs, d_folded, (((0,), (0,)), ((), ())), preferred_element_type=f32)
+    d_slots = jnp.dot(belongs_t[...], d_folded, preferred_element_type=f32)
     dsend[...] = d_slots.astype(bf16).reshape(N_ENC, 16, LANES)
     for p in (5, 4, 3, 2, 1, 0):
         for r in range(2):
@@ -451,8 +456,8 @@
     vy[y] = (vx[0] + vx[1]) + (vx[2] + vx[3])
     for copy in vectors_y:
         copy.start()
+    sum_x(0)
     pass_on(N_PIECES - 1)
-    sum_x(0)
     sum_x(1)
     d_user_vec = lax.dot_general(d_score, embed, (((0,), (0,)), ((), ())), preferred_element_type=f32)
     uvec[...] = (d_user_vec * score_scale).astype(bf16)
@@ -554,6 +559,8 @@
             pltpu.VMEM((USERS_DEV, D), bf16),
             pltpu.VMEM((D, D), bf16),
             pltpu.VMEM((D, D), bf16),
+            pltpu.VMEM((D, USERS_DEV), bf16),
+            pltpu.VMEM((N_ENC * 16, 48), bf16),
             pltpu.VMEM((D, SLOTS * MAIN), bf16),
             pltpu.VMEM((D, 32), bf16),
             pltpu.VMEM((N_PIECES, NX, NY, 16, FOLD), bf16),

time: 95.1 us -> 92.5 us (0.973)
  Pallas kernels: 92.9 us -> 89.9 us
    pallas_call x1, Pallas kernels: 91.1 us -> 88.1 us  [train_step(): pl.pallas_call(step_kernel, out_shape=(jax.ShapeDtypeStruct((USERS_DEV, D...]
where the time goes in v4:
time: 92.5 us; the launch traced here: 91.2 us
  Pallas kernels  89.9 us (97%)
  between operations  1.29 us (1%)
    pallas_call x1, Pallas kernels, train_step(): pl.pallas_call(step_kernel, out_shape=(jax.ShapeDtypeStruct((USERS_DEV, D...  88.1 us

profile of v4, /device:TPU:6, one launch (start us, length us, event | category | flops | bytes accessed | tf_op | source)
XLA Modules:
  0.0 91.2 jit_solution(15695658769217708710)
XLA Ops:
  1.3 88.1 %train_step.1 = (bf16[256,768]{1,0:T(8,128)(2,1)}, f32[12,1,768]{2,1,0:T(1,128)}, f32[1,768]{1,0:T(1,128)}, f32[1,768]{1,0:T(1,128)}) custom-call(s32[16]{0:T(128)} %blocks_ref.1, s32[4]{0:T(128)} %ids_ref.1, s32[1]{0:T(128)S(6)} %copy.15.live_ref, s32[2,128]{1,0:T(2,128)} %bitcast.8, bf16[196,4,768]{2,1,0:T(4,128)(2,1)} %bitcast.5, ...), custom_call_target="tpu_custom_call" | custom-call | tf_op jit(solution)/shard_map/train_step/pallas_call | solution.py:523
  89.4 1.8 %copy_out.1 = (bf16[256,768]{1,0:T(8,128)(2,1)}, f32[12,1,768]{2,1,0:T(1,128)}, f32[1,768]{1,0:T(1,128)}, f32[1,768]{1,0:T(1,128)}) custom-call(bf16[256,768]{1,0:T(8,128)(2,1)} %get-tuple-element.12.refs_0_, f32[12,1,768]{2,1,0:T(1,128)} %get-tuple-element.13.refs_1_, f32[1,768]{1,0:T(1,128)} %get-tuple-element.14.refs_2_, f32[1,768]{1,0:T(1,128)} %get-tuple-element.15.refs_3_), custom_call_target="tpu_custom_call" | custom-call | tf_op jit(solution)/shard_map/copy_out/pallas_call | solution.py:507

commit v5 on v4

--- a/solution.py
+++ b/solution.py
@@ -338,7 +338,8 @@
     dtail[...] = jnp.zeros_like(dtail)
     dbacc[...] = jnp.zeros_like(dbacc)
 
-    def backward(j, carry):
+    def backward(j, done):
+        carry = None
         @pl.when(j > 0)
         def _():
             remote(dsend.at[j], drecv.at[j], sem_ds.at[j], sem_dr.at[j],
@@ -354,9 +355,11 @@
                 rstd = jnp.concatenate([rstd_m[own, rows, :]] * PIECES, axis=1)
                 d_projected = rows_back(u, slope_m[own, rows, :], xhat_m[own, rows, :], rstd)
                 dlow[own, rows, :] = d_projected.astype(bf16)
-                dbacc[...] += d_projected[0:8] + d_projected[8:16]
-        return carry
-    lax.fori_loop(0, N_ENC, backward, 0)
+                part = d_projected[0:8] + d_projected[8:16]
+                carry = part if carry is None else carry + part
+        dbacc[...] += carry
+        return done
+    lax.fori_loop(0, N_ENC, backward, 0, unroll=2)
     for s in range(2):
         rows = slice(s * GROUP, (s + 1) * GROUP)
         rstd = jnp.concatenate([rstd_t[rows, :]] * PIECES, axis=1)
@@ -439,7 +442,7 @@
                 total = sx[h, x, own].astype(f32) + (rx[h, 2 + n, k].astype(f32) + rx[h, 4 + n, k].astype(f32))
                 accx[h, own] = total
                 sy[h, own] = total.astype(bf16)
-        for d in range(1, NY):
+        for d in (4, 3, 5, 2, 6, 1, 7):
             along_y(h, d).start()
 
     def sum_y(h):
@@ -459,19 +462,19 @@
     sum_x(0)
     pass_on(N_PIECES - 1)
     sum_x(1)
-    d_user_vec = lax.dot_general(d_score, embed, (((0,), (0,)), ((), ())), preferred_element_type=f32)
-    uvec[...] = (d_user_vec * score_scale).astype(bf16)
-
-    @pl.loop(0, D // 256)
-    def _(m):
-        lanes = pl.ds(pl.multiple_of(m * 256, 256), 256)
-        duser_ref[:, lanes] = jnp.dot(uvec[...], proj_t[:, lanes], preferred_element_type=f32).astype(bf16)
-
     sum_x(2)
     for copy in vectors_y:
         copy.wait_recv()
     vz[0] = ((vy[0] + vy[1]) + (vy[2] + vy[3])) + ((vy[4] + vy[5]) + (vy[6] + vy[7]))
     vectors_z.start()
+    d_user_vec = lax.dot_general(d_score, embed, (((0,), (0,)), ((), ())), preferred_element_type=f32)
+    uvec[...] = (d_user_vec * score_scale).astype(bf16)
+
+    @pl.loop(0, D // 256)
+    def _(m):
+        lanes = pl.ds(pl.multiple_of(m * 256, 256), 256)
+        duser_ref[:, lanes] = jnp.dot(uvec[...], proj_t[:, lanes], preferred_element_type=f32).astype(bf16)
+
     for h in range(N_PIECES):
         sum_y(h)
     scale = 1.0 / (NX * NY * NZ)
@@ -510,7 +513,7 @@
         in_specs=[pl.BlockSpec(memory_space=pltpu.VMEM)] * len(arrays),
         out_specs=[pl.BlockSpec(memory_space=pl.ANY)] * len(arrays),
         scratch_shapes=[pltpu.SemaphoreType.DMA((len(arrays),))],
-        compiler_params=pltpu.CompilerParams(vmem_limit_bytes=60 * 1024 * 1024),
+        compiler_params=pltpu.CompilerParams(vmem_limit_bytes=2 * 1024 * 1024),
         name="copy_out",
     )(*arrays)
 
@@ -523,10 +526,10 @@
     return pl.pallas_call(
         step_kernel,
         out_shape=(
-            jax.ShapeDtypeStruct((USERS_DEV, D), bf16),
-            jax.ShapeDtypeStruct((ROWS_DEV, 1, D), f32),
-            jax.ShapeDtypeStruct((1, D), f32),
-            jax.ShapeDtypeStruct((1, D), f32),
+            pltpu.VMEM((USERS_DEV, D), bf16),
+            pltpu.VMEM((ROWS_DEV, 1, D), f32),
+            pltpu.VMEM((1, D), f32),
+            pltpu.VMEM((1, D), f32),
         ),
         in_specs=[smem] * 3 + [vmem] * 2 + [anywhere] + [vmem] * 2 + [anywhere] * 3,
         out_specs=[vmem] * 4,

time: 92.5 us -> 90.6 us (0.979)
  Pallas kernels: 89.9 us -> 88 us
    pallas_call x1, Pallas kernels: 1.81 us -> 0.79 us  [copy_out(): pl.pallas_call(copy_kernel, out_shape=[jax.ShapeDtypeStruct(a.shape, a.dt...]
where the time goes in v5:
time: 90.6 us; the launch traced here: 89.3 us
  Pallas kernels  88 us (97%)
  between operations  1.29 us (1%)
    pallas_call x1, Pallas kernels, train_step(): pl.pallas_call(step_kernel, out_shape=(pltpu.VMEM((USERS_DEV, D), bf16),...  87.3 us

profile of v5, /device:TPU:6, one launch (start us, length us, event | category | flops | bytes accessed | tf_op | source)
XLA Modules:
  0.0 89.3 jit_solution(17414604569098515555)
XLA Ops:
  1.3 87.3 %train_step.1 = (bf16[256,768]{1,0:T(8,128)(2,1)S(1)}, f32[12,1,768]{2,1,0:T(1,128)S(1)}, f32[1,768]{1,0:T(1,128)S(1)}, f32[1,768]{1,0:T(1,128)S(1)}) custom-call(s32[16]{0:T(128)} %blocks_ref.1, s32[4]{0:T(128)} %ids_ref.1, s32[1]{0:T(128)S(6)} %copy.15.live_ref, s32[2,128]{1,0:T(2,128)} %bitcast.8, bf16[196,4,768]{2,1,0:T(4,128)(2,1)} %bitcast.5, ...), custom_call_target="tpu_custom_call" | custom-call | tf_op jit(solution)/shard_map/train_step/pallas_call | solution.py:526
  88.5 0.8 copy_out.1

commit v6 on v5

--- a/solution.py
+++ b/solution.py
@@ -258,7 +258,7 @@
             def _():
                 remote(send.at[2 * p + r], recv.at[2 * p + r], sem_s.at[2 * p + r], sem_r.at[2 * p + r],
                        {"enc": (enc // 2) * 2 + 1 - core}).wait_recv()
-        @pl.loop(0, D // 256)
+        @pl.loop(0, D // 256, unroll=True)
         def _(m):
             first = pl.multiple_of(m * 256, 256)
             proj[:, pl.ds(first, 256)] = jnp.dot(
@@ -377,7 +377,7 @@
         copy.start()
 
     def pack(h, xx):
-        @pl.loop(0, NY)
+        @pl.loop(0, NY, unroll=True)
         def _(k):
             first = pl.multiple_of((xx * NY + k) * 24, 8)
             chunk = g[pl.ds(first, 24), :]
@@ -435,7 +435,7 @@
         for n in range(2, 6):
             along_x(h, n).wait_recv()
 
-        @pl.loop(0, NY // 2)
+        @pl.loop(0, NY // 2, unroll=True)
         def _(k):
             for n in range(2):
                 own = k + n * (NY // 2)

time: 90.6 us -> 89.4 us (0.987)
  Pallas kernels: 88 us -> 86.8 us
    pallas_call x1, Pallas kernels: 87.3 us -> 86 us  [train_step(): pl.pallas_call(step_kernel, out_shape=(pltpu.VMEM((USERS_DEV, D), bf16),...]
where the time goes in v6:
time: 89.4 us; the launch traced here: 88.1 us
  Pallas kernels  86.8 us (97%)
  between operations  1.29 us (1%)
    pallas_call x1, Pallas kernels, train_step(): pl.pallas_call(step_kernel, out_shape=(pltpu.VMEM((USERS_DEV, D), bf16),...  86 us

profile of v6, /device:TPU:6, one launch (start us, length us, event | category | flops | bytes accessed | tf_op | source)
XLA Modules:
  0.0 88.1 jit_solution(5544968631390450248)
XLA Ops:
  1.3 86.0 %train_step.1 = (bf16[256,768]{1,0:T(8,128)(2,1)S(1)}, f32[12,1,768]{2,1,0:T(1,128)S(1)}, f32[1,768]{1,0:T(1,128)S(1)}, f32[1,768]{1,0:T(1,128)S(1)}) custom-call(s32[16]{0:T(128)} %blocks_ref.1, s32[4]{0:T(128)} %ids_ref.1, s32[1]{0:T(128)S(6)} %copy.15.live_ref, s32[2,128]{1,0:T(2,128)} %bitcast.8, bf16[196,4,768]{2,1,0:T(4,128)(2,1)} %bitcast.5, ...), custom_call_target="tpu_custom_call" | custom-call | tf_op jit(solution)/shard_map/train_step/pallas_call | solution.py:526
  87.3 0.8 copy_out.1
